TPU v7x, 256 devices: a whole 4x4x8 slice. The times are simulated.
256 devices in a mesh: expert: 64 (over z, x, core), tensor: 4 (over y).
Axes of the slice: x: 4, y: 4, z: 8, core: 2. Of those that a mesh axis runs over, the one named last changes fastest.
Arguments:
- tokens: bfloat16 [16384, 1024], P('expert'), may hold values from -6 to 6
- routes: int32 [16384, 2], P('expert'), may hold values from 0 to 63, all different within a row; in each aligned block of 256 rows (0 to 255, 256 to 511, ...) at most 16 rows name the same one
- mix_weights: float32 [16384, 2], P('expert'), may hold values from 0.2 to 1
- w_gate: bfloat16 [64, 1024, 2048], P('expert', None, 'tensor'), may hold values from -0.1875 to 0.1875
- w_up: bfloat16 [64, 1024, 2048], P('expert', None, 'tensor'), may hold values from -0.1875 to 0.1875
- w_down: bfloat16 [64, 2048, 1024], P('expert', 'tensor'), may hold values from -0.125 to 0.125
- cotangent: bfloat16 [16384, 1024], P('expert'), may hold values from -6 to 6
Outputs:
- result: bfloat16 [16384, 1024], P('expert')
- grad_tokens: bfloat16 [16384, 1024], P('expert')
- grad_gate: float32 [64, 1024, 2048], P('expert', None, 'tensor')
- grad_up: float32 [64, 1024, 2048], P('expert', None, 'tensor')
- grad_down: float32 [64, 2048, 1024], P('expert', 'tensor')
Inputs may be any that keep to these rules, and one draw needn't show every extreme that they name: `routes`: each row names two different experts. Within each aligned block of 256 rows no expert is named by more than 16 rows, a bound that some block reaches.
All inputs are finite; a program needn't handle non-finite values.
Results may differ from a plain program's by a relative error of at most 0.015.
Values may be sent and summed in bfloat16 or wider, within the bound.
No kernel may reach another device: no remote copies, remote signals or barrier semaphores. Data moves between devices by JAX's collectives and lax.ppermute only.
A program may use at most 128 MiB of HBM per device.

v0:
```python
import functools

import jax
import jax.numpy as jnp
from jax import lax
from jax.experimental import pallas as pl
from jax.experimental.pallas import tpu as pltpu
from jax.sharding import PartitionSpec as P

F32 = jnp.float32
BF16 = jnp.bfloat16
NN = (((1,), (0,)), ((), ()))
NT = (((1,), (1,)), ((), ()))
TN = (((0,), (0,)), ((), ()))


def dot(a, b, dims):
    return lax.dot_general(a, b, dims, preferred_element_type=F32)


VMEM = pl.BlockSpec(memory_space=pltpu.VMEM)
SMEM = pl.BlockSpec(memory_space=pltpu.SMEM)
ANY = pl.BlockSpec(memory_space=pl.ANY)
HBM = pl.BlockSpec(memory_space=pltpu.HBM)
TOKEN = jax.ShapeDtypeStruct((8, 128), F32)


def one_hot(place, height):
    lines = lax.broadcasted_iota(jnp.int32, (height, place.shape[1]), 0)
    return (lines == place).astype(F32).astype(BF16)


def dispatch_kernel(capacity, experts, me, routes_in, mix_in, tokens_in, cotangent_in, sent, info, *scratch):
    routes, mix, tokens, cotangent, sems = scratch
    rows, width = tokens.shape
    mine = pl.ds(pl.multiple_of(me[0] * width, width), width)
    fetches = [
        pltpu.make_async_copy(source, slot, sems.at[i])
        for i, (source, slot) in enumerate(
            [
                (routes_in, routes),
                (mix_in, mix),
                (tokens_in.at[:, mine], tokens),
                (cotangent_in.at[:, mine], cotangent),
            ]
        )
    ]
    for fetch in fetches:
        fetch.start()
    for fetch in fetches:
        fetch.wait()
    first, second = routes[0:1, :], routes[1:2, :]
    lines = lax.broadcasted_iota(jnp.int32, (experts, rows), 0)
    hot0 = (lines == first).astype(F32)
    hot1 = (lines == second).astype(F32)
    before = lax.broadcasted_iota(jnp.int32, (rows, rows), 0) < lax.broadcasted_iota(jnp.int32, (rows, rows), 1)
    earlier = dot((hot0 + hot1).astype(BF16), before.astype(F32).astype(BF16), NN)
    rank0 = jnp.sum(earlier * hot0, axis=0, keepdims=True)
    rank1 = jnp.sum((earlier + hot0) * hot1, axis=0, keepdims=True)
    place0 = first * capacity + rank0.astype(jnp.int32)
    place1 = second * capacity + rank1.astype(jnp.int32)
    buffer_rows = experts * capacity
    pick0, pick1 = one_hot(place0, buffer_rows), one_hot(place1, buffer_rows)
    columns = jnp.concatenate(
        [place0.astype(F32), place1.astype(F32), mix[...], jnp.zeros((4, rows), F32)], axis=0
    ).T
    info[...] = columns
    x = dot(pick0 + pick1, tokens[...], NN).astype(BF16)
    sent[:, pl.ds(0, capacity), :] = x.reshape(experts, capacity, x.shape[1])
    cot = cotangent[...].astype(F32)
    scaled0 = (columns[:, 2:3] * cot).astype(BF16)
    scaled1 = (columns[:, 3:4] * cot).astype(BF16)
    g = (dot(pick0, scaled0, NN) + dot(pick1, scaled1, NN)).astype(BF16)
    sent[:, pl.ds(capacity, capacity), :] = g.reshape(experts, capacity, g.shape[1])


def dispatch(me, routes, mix, tokens, cotangent, experts, capacity, parts):
    rows, width = tokens.shape[0], tokens.shape[1] // parts
    return pl.pallas_call(
        functools.partial(dispatch_kernel, capacity, experts),
        in_specs=[SMEM] + [HBM] * 4,
        out_specs=[VMEM] * 2,
        out_shape=(
            jax.ShapeDtypeStruct((experts, 2 * capacity, width), BF16),
            jax.ShapeDtypeStruct((rows, 8), F32),
        ),
        scratch_shapes=[
            pltpu.VMEM((2, rows), jnp.int32),
            pltpu.VMEM((2, rows), F32),
            pltpu.VMEM((rows, width), BF16),
            pltpu.VMEM((rows, width), BF16),
            pltpu.SemaphoreType.DMA((4,)),
        ],
        compiler_params=pltpu.CompilerParams(vmem_limit_bytes=60 << 20),
        name="dispatch",
    )(me, routes.T, mix.T, tokens, cotangent)


def pick_kernel(start, received, after, out):
    out[...] = received[:, pl.ds(start, out.shape[1]), :]


def pick(received, start, capacity, after):
    experts, _, width = received.shape
    return pl.pallas_call(
        functools.partial(pick_kernel, start),
        in_specs=[VMEM, VMEM],
        out_specs=VMEM,
        out_shape=jax.ShapeDtypeStruct((experts, capacity, width), BF16),
        compiler_params=pltpu.CompilerParams(vmem_limit_bytes=2 << 20),
        name="pick",
    )(received, after).reshape(experts * capacity, width)


def column_block(me, shift, parts, width):
    owner = lax.rem(me[0] + (parts - shift), parts)
    return pl.multiple_of(owner * width, width)


def by_chunk(refs, counts, halves):
    chunks, at = [], 0
    for count in counts:
        if count == 1:
            rows = refs[at].shape[0] // halves
            chunks.append([refs[at].at[pl.ds(h * rows, rows), :] for h in range(halves)])
        else:
            chunks.append(list(refs[at : at + count]))
        at += count
    return chunks


def forward_kernel(parts, halves, counts, me, *refs):
    n = sum(counts)
    x = by_chunk(refs[:n], counts, halves)
    w_gate, w_up, w_down = refs[n : n + 3]
    pre_gate, pre_up, hidden = refs[n + 3 : n + 6]
    partial_out = refs[n + 6 :]
    rows, width = partial_out[0].shape
    for h in range(halves):
        gate = up = None
        for shift in range(parts):
            block = x[shift][h][...]
            lines = pl.ds(column_block(me, shift, parts, width), width)
            g = dot(block, w_gate[0, lines, :], NN)
            u = dot(block, w_up[0, lines, :], NN)
            gate, up = (g, u) if gate is None else (gate + g, up + u)
        part = pl.ds(h * rows, rows)
        pre_gate[part, :] = gate
        pre_up[part, :] = up
        act = (gate / (1.0 + jnp.exp(-gate)) * up).astype(BF16)
        hidden[part, :] = act
        for shift in range(parts):
            columns = pl.ds(column_block(me, parts - shift, parts, width), width)
            partial_out[shift * halves + h][...] = dot(act, w_down[0, :, columns], NN).astype(BF16)


def forward(me, x, w_gate, w_up, w_down):
    parts, halves, counts = len(x), 2, tuple(map(len, x))
    rows, width = x[0][0].shape[0] * counts[0] // halves, x[0][0].shape[1]
    units = w_gate.shape[2]
    n = parts * halves
    out = pl.pallas_call(
        functools.partial(forward_kernel, parts, halves, counts),
        in_specs=[SMEM] + [VMEM] * (sum(counts) + 3),
        out_specs=[VMEM] * (n + 3),
        out_shape=[jax.ShapeDtypeStruct((halves * rows, units), F32)] * 2
        + [jax.ShapeDtypeStruct((halves * rows, units), BF16)]
        + [jax.ShapeDtypeStruct((rows, width), BF16)] * n,
        compiler_params=pltpu.CompilerParams(vmem_limit_bytes=10 << 20),
        cost_estimate=pl.CostEstimate(
            flops=6 * halves * rows * parts * width * units, bytes_accessed=12 << 20, transcendentals=halves * rows * units
        ),
        name="forward",
    )(me, *[piece for chunk in x for piece in chunk], w_gate, w_up, w_down)
    return out[0], out[1], out[2], [out[3 + i * halves : 3 + (i + 1) * halves] for i in range(parts)]


def backward_kernel(parts, halves, counts, me, *refs):
    n = sum(counts)
    g = by_chunk(refs[:n], counts, halves)
    pre_gate, pre_up, w_gate, w_up, w_down = refs[n : n + 5]
    d_gate, d_up, done = refs[n + 5 : n + 8]
    partial_in = refs[n + 8 :]
    done[...] = jnp.zeros(done.shape, F32)
    rows, width = partial_in[0].shape
    for h in range(halves):
        d_hidden = None
        for shift in range(parts):
            columns = pl.ds(column_block(me, shift, parts, width), width)
            part = dot(g[shift][h][...], w_down[0, :, columns], NT)
            d_hidden = part if d_hidden is None else d_hidden + part
        mine = pl.ds(h * rows, rows)
        gate, up = pre_gate[mine, :], pre_up[mine, :]
        sigma = 1.0 / (1.0 + jnp.exp(-gate))
        dg = (d_hidden * up * sigma * (1.0 + gate * (1.0 - sigma))).astype(BF16)
        du = (d_hidden * gate * sigma).astype(BF16)
        d_gate[mine, :] = dg
        d_up[mine, :] = du
        for shift in range(parts):
            lines = pl.ds(column_block(me, parts - shift, parts, width), width)
            partial_in[shift * halves + h][...] = (
                dot(dg, w_gate[0, lines, :], NT) + dot(du, w_up[0, lines, :], NT)
            ).astype(BF16)


def backward(me, g, pre_gate, pre_up, w_gate, w_up, w_down):
    parts, halves, counts = len(g), 2, tuple(map(len, g))
    rows, width = g[0][0].shape[0] * counts[0] // halves, g[0][0].shape[1]
    units = w_gate.shape[2]
    n = parts * halves
    out = pl.pallas_call(
        functools.partial(backward_kernel, parts, halves, counts),
        in_specs=[SMEM] + [VMEM] * (sum(counts) + 5),
        out_specs=[VMEM] * (n + 3),
        out_shape=[jax.ShapeDtypeStruct((halves * rows, units), BF16)] * 2
        + [TOKEN]
        + [jax.ShapeDtypeStruct((rows, width), BF16)] * n,
        compiler_params=pltpu.CompilerParams(vmem_limit_bytes=10 << 20),
        cost_estimate=pl.CostEstimate(
            flops=6 * halves * rows * parts * width * units, bytes_accessed=12 << 20, transcendentals=halves * rows * units
        ),
        name="backward",
    )(me, *[piece for chunk in g for piece in chunk], pre_gate, pre_up, w_gate, w_up, w_down)
    return out[0], out[1], out[2], [out[3 + i * halves : 3 + (i + 1) * halves] for i in range(parts)]


def weights_kernel(parts, counts, me, *refs):
    n = sum(counts)
    sources = refs[: 2 * n + 3]
    grad_gate, grad_up, grad_down, done = refs[2 * n + 4 : 2 * n + 8]
    x, g, units_in, tall, wide, in_sems, out_sems = refs[2 * n + 8 :]
    rows, width = x.shape[1:]
    done[...] = jnp.zeros(done.shape, F32)

    def fetch(kind, shift):
        first = kind * n + sum(counts[:shift])
        size = rows // counts[shift]
        return [
            pltpu.make_async_copy(
                sources[first + i], (x, g)[kind].at[shift, pl.ds(i * size, size), :], in_sems.at[first + i]
            )
            for i in range(counts[shift])
        ]

    units = [
        pltpu.make_async_copy(sources[2 * n + i], units_in.at[i], in_sems.at[2 * n + i]) for i in range(3)
    ]
    stages = [[units[1]] + fetch(0, 0), [units[2]]]
    stages += [fetch(0, shift) for shift in range(1, parts)]
    stages += [[units[0]] + fetch(1, 0)] + [fetch(1, shift) for shift in range(1, parts)]
    for stage in stages:
        for copy in stage:
            copy.start()

    def arrived(stage):
        for copy in stages[stage]:
            copy.wait()

    copies = []

    def send(kind, shift, slot, target):
        copy = pltpu.make_async_copy(slot, target, out_sems.at[kind * parts + shift])
        copy.start()
        copies.append(copy)

    for shift in range(parts):
        where = pl.ds(column_block(me, shift, parts, width), width)
        arrived(0 if shift == 0 else 1 + shift)
        tall[shift] = dot(x[shift], units_in[1], TN)
        send(0, shift, tall.at[shift], grad_gate.at[0, where, :])
        if shift == 0:
            arrived(1)
        tall[parts + shift] = dot(x[shift], units_in[2], TN)
        send(1, shift, tall.at[parts + shift], grad_up.at[0, where, :])
    for shift in range(parts):
        where = pl.ds(column_block(me, shift, parts, width), width)
        arrived(1 + parts + shift)
        wide[shift] = dot(units_in[0], g[shift], TN)
        send(2, shift, wide.at[shift], grad_down.at[0, :, where])
    for copy in copies:
        copy.wait()


def weight_grads(me, x, g, hidden, d_gate, d_up, after):
    parts, counts = len(x), tuple(map(len, x))
    rows, width = x[0][0].shape[0] * counts[0], x[0][0].shape[1]
    units = hidden.shape[1]
    n = sum(counts)
    return pl.pallas_call(
        functools.partial(weights_kernel, parts, counts),
        in_specs=[SMEM] + [HBM] * (2 * n + 3) + [VMEM],
        out_specs=[HBM] * 3 + [VMEM],
        out_shape=(
            jax.ShapeDtypeStruct((1, parts * width, units), F32),
            jax.ShapeDtypeStruct((1, parts * width, units), F32),
            jax.ShapeDtypeStruct((1, units, parts * width), F32),
            TOKEN,
        ),
        scratch_shapes=[
            pltpu.VMEM((parts, rows, width), BF16),
            pltpu.VMEM((parts, rows, width), BF16),
            pltpu.VMEM((3, rows, units), BF16),
            pltpu.VMEM((2 * parts, width, units), F32),
            pltpu.VMEM((parts, units, width), F32),
            pltpu.SemaphoreType.DMA((2 * n + 3,)),
            pltpu.SemaphoreType.DMA((3 * parts,)),
        ],
        compiler_params=pltpu.CompilerParams(vmem_limit_bytes=58 << 20),
        cost_estimate=pl.CostEstimate(
            flops=6 * rows * parts * width * units, bytes_accessed=13 << 20, transcendentals=0
        ),
        name="weight_grads",
    )(me, *[v for c in x for v in c], *[v for c in g for v in c], hidden, d_gate, d_up, after)


def total_kernel(halves, *refs):
    out, done = refs[-2:]
    terms = len(refs[:-3]) // halves
    done[...] = jnp.zeros(done.shape, F32)
    rows = refs[0].shape[0]
    step = 32

    @pl.loop(0, rows // step)
    def _(i):
        here = pl.ds(pl.multiple_of(i * step, step), step)
        for h in range(halves):
            total = refs[h * terms][here, :].astype(F32)
            for k in range(1, terms):
                total = total + refs[h * terms + k][here, :].astype(F32)
            out[pl.ds(pl.multiple_of(h * rows + i * step, step), step), :] = total.astype(BF16)


def totals(groups, after):
    rows, width = groups[0][0].shape
    return pl.pallas_call(
        functools.partial(total_kernel, len(groups)),
        in_specs=[VMEM] * sum(map(len, groups)) + [VMEM],
        out_specs=[VMEM] * 2,
        out_shape=(jax.ShapeDtypeStruct((len(groups) * rows, width), BF16), TOKEN),
        compiler_params=pltpu.CompilerParams(vmem_limit_bytes=2 << 20),
        name="totals",
    )(*[v for group in groups for v in group], after)


def assemble_kernel(parts, me, *refs):
    out, done, sems = refs[parts:]
    done[...] = jnp.zeros(done.shape, F32)
    width = refs[0].shape[1]
    copies = []
    for shift in range(parts):
        columns = pl.ds(column_block(me, shift, parts, width), width)
        copies.append(pltpu.make_async_copy(refs[shift], out.at[:, columns], sems.at[shift]))
        copies[-1].start()
    for copy in copies:
        copy.wait()


def assemble(me, chunks):
    rows, width = chunks[0].shape
    parts = len(chunks)
    return pl.pallas_call(
        functools.partial(assemble_kernel, parts),
        in_specs=[SMEM] + [VMEM] * parts,
        out_specs=[HBM, VMEM],
        out_shape=(jax.ShapeDtypeStruct((rows, width * parts), BF16), TOKEN),
        scratch_shapes=[pltpu.SemaphoreType.DMA((parts,))],
        compiler_params=pltpu.CompilerParams(vmem_limit_bytes=2 << 20),
        name="assemble",
    )(me, *chunks)


def combine_kernel(weighted, info, back, *refs):
    out = refs[-1]
    values = back[...]
    columns = info[...]
    lanes = lax.broadcasted_iota(jnp.int32, (columns.shape[0], values.shape[0]), 1)
    picked = []
    for k in range(2):
        hot = (lanes == columns[:, k : k + 1].astype(jnp.int32)).astype(F32).astype(BF16)
        row = dot(hot, values, NN)
        picked.append(row * columns[:, 2 + k : 3 + k] if weighted else row)
    out[...] = (picked[0] + picked[1]).astype(BF16)


def combine(info, back, weighted, after):
    return pl.pallas_call(
        functools.partial(combine_kernel, weighted),
        in_specs=[VMEM] * (2 + len(after)),
        out_specs=VMEM,
        out_shape=jax.ShapeDtypeStruct((info.shape[0], back.shape[1]), BF16),
        compiler_params=pltpu.CompilerParams(vmem_limit_bytes=8 << 20),
        name="combine",
    )(info, back, *after)


def swap_blocks(values):
    return lax.all_to_all(values, "expert", split_axis=0, concat_axis=0, tiled=True)


def send_back(values, experts, capacity):
    rows, width = values.shape
    return swap_blocks(values.reshape(experts, capacity, width)).reshape(rows, width)


def shift_by(values, step):
    size = lax.axis_size("tensor")
    return lax.ppermute(values, "tensor", [(i, (i + step) % size) for i in range(size)])


def gather_ring(own):
    rows = own.shape[0] // 2
    left = shift_by(own, 1)
    right = shift_by(own, -1)
    far_top = shift_by(left[:rows], 1)
    far_bottom = shift_by(right[rows:], -1)
    return [(own,), (left,), (far_top, far_bottom), (right,)]


def add(a, b):
    return (a.astype(F32) + b.astype(F32)).astype(BF16)


def scatter_ring(chunks):
    own, right, far, left = chunks
    far_top = shift_by(far[0], -1)
    far_bottom = shift_by(far[1], 1)
    from_left_top = shift_by(right[0], 1)
    from_right_bottom = shift_by(left[1], -1)
    from_right_top = shift_by(add(left[0], far_top), -1)
    from_left_bottom = shift_by(add(right[1], far_bottom), 1)
    return [
        (own[0], from_left_top, from_right_top),
        (own[1], from_right_bottom, from_left_bottom),
    ]


def gather_columns(me, values):
    far = shift_by(values, 2)
    left = shift_by(values, 1)
    right = shift_by(values, -1)
    return assemble(me, [values, left, far, right])


def shards(tokens, routes, mix_weights, w_gate, w_up, w_down, cotangent):
    experts = lax.axis_size("expert")
    parts = lax.axis_size("tensor")
    capacity = 4 * tokens.shape[0] // experts
    me = lax.axis_index("tensor").astype(jnp.int32).reshape(1)
    sent, info = dispatch(me, routes, mix_weights, tokens, cotangent, experts, capacity, parts)
    received = swap_blocks(sent)
    x = gather_ring(pick(received, 0, capacity, info))
    g = gather_ring(pick(received, capacity, capacity, info))
    pre_gate, pre_up, hidden, partial_out = forward(me, x, w_gate, w_up, w_down)
    out_terms = scatter_ring(partial_out)
    d_gate, d_up, after_backward, partial_in = backward(me, g, pre_gate, pre_up, w_gate, w_up, w_down)
    out_mine, _ = totals(out_terms, after_backward)
    out_back = send_back(out_mine, experts, capacity)
    in_mine, after_sums = totals(scatter_ring(partial_in), after_backward)
    in_back = send_back(in_mine, experts, capacity)
    grad_gate, grad_up, grad_down, after_weights = weight_grads(me, x, g, hidden, d_gate, d_up, after_sums)
    result, after_result = gather_columns(me, combine(info, out_back, True, [after_sums]))
    grad_tokens, _ = gather_columns(me, combine(info, in_back, False, [after_weights, after_result]))
    return (result, grad_tokens, grad_gate, grad_up, grad_down)


def solution(mesh):
    in_specs = (
        P("expert", None),
        P("expert", None),
        P("expert", None),
        P("expert", None, "tensor"),
        P("expert", None, "tensor"),
        P("expert", "tensor", None),
        P("expert", None),
    )
    out_specs = (
        P("expert", None),
        P("expert", None),
        P("expert", None, "tensor"),
        P("expert", None, "tensor"),
        P("expert", "tensor", None),
    )
    return jax.shard_map(shards, mesh=mesh, in_specs=in_specs, out_specs=out_specs, check_vma=False)
```

profile of v0, /device:TPU:1, one launch (start us, length us, event | category | flops | bytes accessed | tf_op | source)
XLA Modules:
  0.0 175.0 jit_solution(3502598582085501831)
XLA Ops:
  0.6 3.1 %dispatch.1 = (bf16[64,32,256]{2,1,0:T(8,128)(2,1)}, f32[256,8]{1,0:T(8,128)}) custom-call(s32[1]{0:T(128)} %bitcast.me, s32[2,256]{1,0:T(2,128)} %bitcast.19, f32[2,256]{1,0:T(2,128)} %bitcast.20, bf16[256,1024]{1,0:T(8,128)(2,1)} %tokens_in.1, bf16[256,1024]{1,0:T(8,128)(2,1)} %cotangent_in.1), custom_call_target="tpu_custom_call" | custom-call | tf_op jit(solution)/shard_map/dispatch/pallas_call | solution.py:79
  3.8 0.0 copy-start
  3.8 41.1 %all_to_all.15.received = bf16[64,32,256]{2,1,0:T(8,128)(2,1)S(1)} all-to-all(bf16[64,32,256]{2,1,0:T(8,128)(2,1)} %get-tuple-element.40), channel_id=1, replica_groups=mesh['expert'=64,'tensor'=4] {'expert'}, dimensions={0} | all-to-all | bytes 2097152 | tf_op jit(solution)/shard_map/all_to_all | solution.py:397
  44.9 0.0 copy-start.1
  45.0 2.8 %collective-permute-start.2 = (bf16[1024,256]{1,0:T(8,128)(2,1)S(1)}, bf16[1024,256]{1,0:T(8,128)(2,1)S(1)}, u32[]{:S(2)}, u32[]{:S(2)}) collective-permute-start(bf16[1024,256]{1,0:T(8,128)(2,1)S(1)} %bitcast.11), channel_id=1, source_target_pairs={{0,3},{1,0},{2,1},{3,2},{4,7},{5,4},{6,5},{7,6},{8,11},{9,8},{10,9... | collective-permute-start | bytes 1572872 | tf_op jit(solution)/shard_map/ppermute | solution.py:407
  47.8 9.9 %collective-permute-done.2.refs_4_ = bf16[1024,256]{1,0:T(8,128)(2,1)S(1)} collective-permute-done((bf16[1024,256]{1,0:T(8,128)(2,1)S(1)}, bf16[1024,256]{1,0:T(8,128)(2,1)S(1)}, u32[]{:S(2)}, u32[]{:S(2)}) %collective-permute-start.2) | collective-permute-done | bytes 524320 | tf_op jit(solution)/shard_map/ppermute | solution.py:407
  57.6 3.5 %collective-permute-start.3 = (bf16[512,256]{1,0:T(8,128)(2,1)S(1)}, bf16[512,256]{1,0:T(8,128)(2,1)S(1)}, u32[]{:S(2)}, u32[]{:S(2)}) collective-permute-start(bf16[512,256]{1,0:T(8,128)(2,1)S(1)} %slice.17), channel_id=1, source_target_pairs={{0,3},{1,0},{2,1},{3,2},{4,7},{5,4},{6,5},{7,6},{8,11},{9,8},{10,9... | collective-permute-start | bytes 786440 | tf_op jit(solution)/shard_map/ppermute | solution.py:407
  61.1 0.0 collective-permute-done.refs_1_
  61.2 0.1 collective-permute-start.1
  61.3 2.7 %collective-permute-start.12 = (bf16[1024,256]{1,0:T(8,128)(2,1)S(1)}, bf16[1024,256]{1,0:T(8,128)(2,1)S(1)}, u32[]{:S(2)}, u32[]{:S(2)}) collective-permute-start(bf16[1024,256]{1,0:T(8,128)(2,1)S(1)} %bitcast.15), channel_id=1, source_target_pairs={{0,3},{1,0},{2,1},{3,2},{4,7},{5,4},{6,5},{7,6},{8,11},{9,8},{10,9... | collective-permute-start | bytes 1572872 | tf_op jit(solution)/shard_map/ppermute | solution.py:407
  64.0 0.0 collective-permute-start.10
  64.0 0.4 collective-permute-done.3.refs_3_
  64.5 3.2 %collective-permute-done.1.refs_2_ = bf16[512,256]{1,0:T(8,128)(2,1)S(1)} collective-permute-done((bf16[512,256]{1,0:T(8,128)(2,1)S(1)}, bf16[512,256]{1,0:T(8,128)(2,1)S(1)}, u32[]{:S(2)}, u32[]{:S(2)}) %collective-permute-start.1) | collective-permute-done | bytes 262176 | tf_op jit(solution)/shard_map/ppermute | solution.py:407
  67.7 4.0 %forward.1 = (f32[1024,512]{1,0:T(8,128)S(1)}, f32[1024,512]{1,0:T(8,128)S(1)}, bf16[1024,512]{1,0:T(8,128)(2,1)S(1)}, bf16[512,256]{1,0:T(8,128)(2,1)S(1)}, bf1...) custom-call(s32[1]{0:T(128)} %bitcast.me, ...), custom_call_target="tpu_custom_call" | custom-call | flops 3221225472 | bytes 12582912 | tf_op jit(solution)/shard_map/forward/pallas_call | solution.py:162
  71.8 1.0 copy-done.19
  72.8 0.0 collective-permute-start.5
  72.8 1.5 collective-permute-start.8
  74.3 1.5 collective-permute-done.12.refs_4_.refs_9_
  75.8 3.5 %collective-permute-start.13 = (bf16[512,256]{1,0:T(8,128)(2,1)S(1)}, bf16[512,256]{1,0:T(8,128)(2,1)S(1)}, u32[]{:S(2)}, u32[]{:S(2)}) collective-permute-start(bf16[512,256]{1,0:T(8,128)(2,1)S(1)} %slice.19), channel_id=1, source_target_pairs={{0,3},{1,0},{2,1},{3,2},{4,7},{5,4},{6,5},{7,6},{8,11},{9,8},{10,9... | collective-permute-start | bytes 786440 | tf_op jit(solution)/shard_map/ppermute | solution.py:407
  79.3 0.0 collective-permute-done.10.refs_1_.refs_6_
  79.3 0.3 collective-permute-start.11
  79.6 0.1 collective-permute-start.4
  79.7 1.7 collective-permute-done.5
  81.4 3.4 %collective-permute-start.7 = (bf16[512,256]{1,0:T(8,128)(2,1)S(1)}, bf16[512,256]{1,0:T(8,128)(2,1)S(1)}, u32[]{:S(2)}, u32[]{:S(2)}) collective-permute-start(bf16[512,256]{1,0:T(8,128)(2,1)S(1)} %get-tuple-element.46), channel_id=1, source_target_pairs={{0,3},{1,0},{2,1},{3,2},{4,7},{5,4},{6,5},{7,6},{8,11},{9,8},{10,9... | collective-permute-start | bytes 786440 | tf_op jit(solution)/shard_map/ppermute | solution.py:407
  84.8 0.1 add_convert_fusion.3
  84.9 0.1 collective-permute-start.6
  85.0 0.1 add_convert_fusion.2
  85.1 2.0 %collective-permute-done.13.refs_3_.refs_8_ = bf16[512,256]{1,0:T(8,128)(2,1)S(1)} collective-permute-done((bf16[512,256]{1,0:T(8,128)(2,1)S(1)}, bf16[512,256]{1,0:T(8,128)(2,1)S(1)}, u32[]{:S(2)}, u32[]{:S(2)}) %collective-permute-start.13) | collective-permute-done | bytes 262176 | tf_op jit(solution)/shard_map/ppermute | solution.py:407
  87.0 3.1 %collective-permute-done.11.refs_2_.refs_7_ = bf16[512,256]{1,0:T(8,128)(2,1)S(1)} collective-permute-done((bf16[512,256]{1,0:T(8,128)(2,1)S(1)}, bf16[512,256]{1,0:T(8,128)(2,1)S(1)}, u32[]{:S(2)}, u32[]{:S(2)}) %collective-permute-start.11) | collective-permute-done | bytes 262176 | tf_op jit(solution)/shard_map/ppermute | solution.py:407
  90.2 3.8 %backward.1 = (bf16[1024,512]{1,0:T(8,128)(2,1)S(1)}, bf16[1024,512]{1,0:T(8,128)(2,1)S(1)}, f32[8,128]{1,0:T(8,128)S(1)}, bf16[512,256]{1,0:T(8,128)(2,1)S(1)},...) custom-call(s32[1]{0:T(128)} %bitcast.me, ...), custom_call_target="tpu_custom_call" | custom-call | flops 3221225472 | bytes 12582912 | tf_op jit(solution)/shard_map/backward/pallas_call | solution.py:211
  94.1 1.0 copy-done.18
  95.0 0.7 collective-permute-done.4.refs_1_
  95.8 2.5 %collective-permute-done.6.refs_2_ = bf16[512,256]{1,0:T(8,128)(2,1)S(1)} collective-permute-done((bf16[512,256]{1,0:T(8,128)(2,1)S(1)}, bf16[512,256]{1,0:T(8,128)(2,1)S(1)}, u32[]{:S(2)}, u32[]{:S(2)}) %collective-permute-start.6) | collective-permute-done | bytes 262176 | tf_op jit(solution)/shard_map/ppermute | solution.py:407
  98.3 3.1 %collective-permute-done.9.refs_5_ = bf16[512,256]{1,0:T(8,128)(2,1)S(1)} collective-permute-done((bf16[512,256]{1,0:T(8,128)(2,1)S(1)}, bf16[512,256]{1,0:T(8,128)(2,1)S(1)}, u32[]{:S(2)}, u32[]{:S(2)}) %collective-permute-start.9) | collective-permute-done | bytes 262176 | tf_op jit(solution)/shard_map/ppermute | solution.py:407
  101.4 1.1 totals.2
  102.5 10.2 %all-to-all-start.1 = ((bf16[64,16,256]{2,1,0:T(8,128)(2,1)}), bf16[64,16,256]{2,1,0:T(8,128)(2,1)S(1)}, u32[]{:S(2)}, u32[]{:S(2)}) async-start(bf16[64,16,256]{2,1,0:T(8,128)(2,1)} %bitcast.5), calls=%async_computation.1 | async-start | bytes 1048576 | tf_op jit(solution)/shard_map/all_to_all | solution.py:397
  112.7 0.1 collective-permute-start.15
  112.8 1.5 collective-permute-start.18
  114.2 0.0 collective-permute-start.14
  114.2 2.6 %collective-permute-start.17 = (bf16[512,256]{1,0:T(8,128)(2,1)S(1)}, bf16[512,256]{1,0:T(8,128)(2,1)S(1)}, u32[]{:S(2)}, u32[]{:S(2)}) collective-permute-start(bf16[512,256]{1,0:T(8,128)(2,1)S(1)} %get-tuple-element.58), channel_id=1, source_target_pairs={{0,3},{1,0},{2,1},{3,2},{4,7},{5,4},{6,5},{7,6},{8,11},{9,8},{10,9... | collective-permute-start | bytes 786440 | tf_op jit(solution)/shard_map/ppermute | solution.py:407
  116.9 3.5 %collective-permute-done.15 = bf16[512,256]{1,0:T(8,128)(2,1)S(1)} collective-permute-done((bf16[512,256]{1,0:T(8,128)(2,1)}, bf16[512,256]{1,0:T(8,128)(2,1)S(1)}, u32[]{:S(2)}, u32[]{:S(2)}) %collective-permute-start.15) | collective-permute-done | bytes 262176 | tf_op jit(solution)/shard_map/ppermute | solution.py:407
  120.4 0.1 add_convert_fusion.1
  120.5 1.4 collective-permute-start.16
  121.9 0.1 add_convert_fusion
  121.9 0.2 collective-permute-start.19
  122.1 4.8 %collective-permute-done.14.refs_1_ = bf16[512,256]{1,0:T(8,128)(2,1)S(1)} collective-permute-done((bf16[512,256]{1,0:T(8,128)(2,1)S(1)}, bf16[512,256]{1,0:T(8,128)(2,1)S(1)}, u32[]{:S(2)}, u32[]{:S(2)}) %collective-permute-start.14) | collective-permute-done | bytes 262176 | tf_op jit(solution)/shard_map/ppermute | solution.py:407
  127.0 4.6 %collective-permute-done.16.refs_2_ = bf16[512,256]{1,0:T(8,128)(2,1)S(1)} collective-permute-done((bf16[512,256]{1,0:T(8,128)(2,1)S(1)}, bf16[512,256]{1,0:T(8,128)(2,1)S(1)}, u32[]{:S(2)}, u32[]{:S(2)}) %collective-permute-start.16) | collective-permute-done | bytes 262176 | tf_op jit(solution)/shard_map/ppermute | solution.py:407
  131.6 1.0 collective-permute-done.19.refs_5_
  132.6 1.0 totals.3
  133.6 11.3 %all-to-all-start.2 = ((bf16[64,16,256]{2,1,0:T(8,128)(2,1)}), bf16[64,16,256]{2,1,0:T(8,128)(2,1)S(1)}, u32[]{:S(2)}, u32[]{:S(2)}) async-start(bf16[64,16,256]{2,1,0:T(8,128)(2,1)} %bitcast.7), calls=%async_computation.2 | async-start | bytes 1048576 | tf_op jit(solution)/shard_map/all_to_all | solution.py:397
  145.0 0.5 combine.2.refs_0_
  145.5 0.2 collective-permute-start.22
  145.7 1.8 %collective-permute-start.21 = (bf16[256,256]{1,0:T(8,128)(2,1)S(1)}, bf16[256,256]{1,0:T(8,128)(2,1)S(1)}, u32[]{:S(2)}, u32[]{:S(2)}) collective-permute-start(bf16[256,256]{1,0:T(8,128)(2,1)S(1)} %combine.2.refs_0_), channel_id=1, source_target_pairs={{0,2},{1,3},{2,0},{3,1},{4,6},{5,7},{6,4},{7,5},{8,10},{9,11},{10,... | collective-permute-start | bytes 393224 | tf_op jit(solution)/shard_map/ppermute | solution.py:407
  147.5 9.6 %weight_grads.1 = (f32[1,1024,512]{2,1,0:T(8,128)}, f32[1,1024,512]{2,1,0:T(8,128)}, f32[1,512,1024]{2,1,0:T(8,128)}, f32[8,128]{1,0:T(8,128)}) custom-call(s32[1]{0:T(128)} %bitcast.me, bf16[1024,256]{1,0:T(8,128)(2,1)} %bitcast.14, bf16[1024,256]{1,0:T(8,128)(2,1)} %copy-done.4, bf16[512,256]{1,0:T(8,128)(2,1)} %copy-done.13, bf16[512,256]{1,0:T(8,128)(2,1)} %copy-done.12, ...), custom_call_target="tpu_custom_call" | custom-call | flops 3221225472 | bytes 13631488 | tf_op jit(solution)/shard_map/weight_grads/pallas_call | solution.py:289
  157.2 0.8 assemble.2
  158.0 4.7 %all-to-all-done.2 = bf16[64,16,256]{2,1,0:T(8,128)(2,1)S(1)} async-done(((bf16[64,16,256]{2,1,0:T(8,128)(2,1)}), bf16[64,16,256]{2,1,0:T(8,128)(2,1)S(1)}, u32[]{:S(2)}, u32[]{:S(2)}) %all-to-all-start.2) | async-done | bytes 524320 | tf_op jit(solution)/shard_map/all_to_all | solution.py:397
  162.7 0.7 copy-done.8
  163.4 0.5 combine.3.refs_0_
  163.9 0.2 collective-permute-start.25
  164.1 1.8 %collective-permute-start.24 = (bf16[256,256]{1,0:T(8,128)(2,1)S(1)}, bf16[256,256]{1,0:T(8,128)(2,1)S(1)}, u32[]{:S(2)}, u32[]{:S(2)}) collective-permute-start(bf16[256,256]{1,0:T(8,128)(2,1)S(1)} %combine.3.refs_0_), channel_id=1, source_target_pairs={{0,2},{1,3},{2,0},{3,1},{4,6},{5,7},{6,4},{7,5},{8,10},{9,11},{10,... | collective-permute-start | bytes 393224 | tf_op jit(solution)/shard_map/ppermute | solution.py:407
  165.9 2.7 %collective-permute-done.25.refs_3_ = bf16[256,256]{1,0:T(8,128)(2,1)S(1)} collective-permute-done((bf16[256,256]{1,0:T(8,128)(2,1)S(1)}, bf16[256,256]{1,0:T(8,128)(2,1)S(1)}, u32[]{:S(2)}, u32[]{:S(2)}) %collective-permute-start.25) | collective-permute-done | bytes 131104 | tf_op jit(solution)/shard_map/ppermute | solution.py:407
  168.7 1.3 collective-permute-done.24.refs_2_
  170.0 3.4 %collective-permute-done.23.refs_1_ = bf16[256,256]{1,0:T(8,128)(2,1)S(1)} collective-permute-done((bf16[256,256]{1,0:T(8,128)(2,1)S(1)}, bf16[256,256]{1,0:T(8,128)(2,1)S(1)}, u32[]{:S(2)}, u32[]{:S(2)}) %collective-permute-start.23) | collective-permute-done | bytes 131104 | tf_op jit(solution)/shard_map/ppermute | solution.py:407
  173.4 1.4 assemble.3
  (53 shorter events, 0.2 us)
Async XLA Ops:
  3.8 41.1 %copy-start = (f32[256,8]{1,0:T(8,128)S(1)}, f32[256,8]{1,0:T(8,128)}, u32[]{:S(2)}) copy-start(f32[256,8]{1,0:T(8,128)} %get-tuple-element.39.after.info) | copy-start | bytes 24580
  44.9 22.8 %copy-start.9 = (bf16[1,1024,512]{2,1,0:T(8,128)(2,1)S(1)}, bf16[1,1024,512]{2,1,0:T(8,128)(2,1)}, u32[]{:S(2)}) copy-start(bf16[1,1024,512]{2,1,0:T(8,128)(2,1)} %refs_7_.3) | copy-start | bytes 3145732
  44.9 22.8 %copy-start.10 = (bf16[1,1024,512]{2,1,0:T(8,128)(2,1)S(1)}, bf16[1,1024,512]{2,1,0:T(8,128)(2,1)}, u32[]{:S(2)}) copy-start(bf16[1,1024,512]{2,1,0:T(8,128)(2,1)} %refs_8_.1) | copy-start | bytes 3145732
  44.9 22.8 %copy-start.11 = (bf16[1,512,1024]{2,1,0:T(8,128)(2,1)S(1)}, bf16[1,512,1024]{2,1,0:T(8,128)(2,1)}, u32[]{:S(2)}) copy-start(bf16[1,512,1024]{2,1,0:T(8,128)(2,1)} %refs_9_.1) | copy-start | bytes 3145732
  44.9 26.8 %copy-start.1 = (bf16[64,16,256]{2,1,0:T(8,128)(2,1)}, bf16[64,16,256]{2,1,0:T(8,128)(2,1)S(1)}, u32[]{:S(2)}) copy-start(bf16[64,16,256]{2,1,0:T(8,128)(2,1)S(1)} %pick.2) | copy-start | bytes 1572868
  45.0 12.7 %collective-permute-start.2 = (bf16[1024,256]{1,0:T(8,128)(2,1)S(1)}, bf16[1024,256]{1,0:T(8,128)(2,1)S(1)}, u32[]{:S(2)}, u32[]{:S(2)}) collective-permute-start(bf16[1024,256]{1,0:T(8,128)(2,1)S(1)} %bitcast.11), channel_id=1, source_target_pairs={{0,3},{1,0},{2,1},{3,2},{4,7},{5,4},{6,5},{7,6},{8,11},{9,8},{10,9... | collective-permute-start | bytes 1572872 | tf_op jit(solution)/shard_map/ppermute | solution.py:407
  47.8 13.4 %collective-permute-start = (bf16[1024,256]{1,0:T(8,128)(2,1)S(1)}, bf16[1024,256]{1,0:T(8,128)(2,1)S(1)}, u32[]{:S(2)}, u32[]{:S(2)}) collective-permute-start(bf16[1024,256]{1,0:T(8,128)(2,1)S(1)} %bitcast.12), channel_id=1, source_target_pairs={{0,1},{1,2},{2,3},{3,0},{4,5},{5,6},{6,7},{7,4},{8,9},{9,10},{10,1... | collective-permute-start | bytes 1572872 | tf_op jit(solution)/shard_map/ppermute | solution.py:407
  57.6 14.1 %copy-start.3 = (bf16[1024,256]{1,0:T(8,128)(2,1)}, bf16[1024,256]{1,0:T(8,128)(2,1)S(1)}, u32[]{:S(2)}) copy-start(bf16[1024,256]{1,0:T(8,128)(2,1)S(1)} %collective-permute-done.2.refs_4_) | copy-start | bytes 1572868
  57.6 6.8 %collective-permute-start.3 = (bf16[512,256]{1,0:T(8,128)(2,1)S(1)}, bf16[512,256]{1,0:T(8,128)(2,1)S(1)}, u32[]{:S(2)}, u32[]{:S(2)}) collective-permute-start(bf16[512,256]{1,0:T(8,128)(2,1)S(1)} %slice.17), channel_id=1, source_target_pairs={{0,3},{1,0},{2,1},{3,2},{4,7},{5,4},{6,5},{7,6},{8,11},{9,8},{10,9... | collective-permute-start | bytes 786440 | tf_op jit(solution)/shard_map/ppermute | solution.py:407
  61.1 10.6 %copy-start.4 = (bf16[1024,256]{1,0:T(8,128)(2,1)}, bf16[1024,256]{1,0:T(8,128)(2,1)S(1)}, u32[]{:S(2)}) copy-start(bf16[1024,256]{1,0:T(8,128)(2,1)S(1)} %collective-permute-done.refs_1_) | copy-start | bytes 1572868
  61.2 6.5 %collective-permute-start.1 = (bf16[512,256]{1,0:T(8,128)(2,1)S(1)}, bf16[512,256]{1,0:T(8,128)(2,1)S(1)}, u32[]{:S(2)}, u32[]{:S(2)}) collective-permute-start(bf16[512,256]{1,0:T(8,128)(2,1)S(1)} %slice.16), channel_id=1, source_target_pairs={{0,1},{1,2},{2,3},{3,0},{4,5},{5,6},{6,7},{7,4},{8,9},{9,10},{10,1... | collective-permute-start | bytes 786440 | tf_op jit(solution)/shard_map/ppermute | solution.py:407
  61.3 28.9 %copy-start.2 = (bf16[64,16,256]{2,1,0:T(8,128)(2,1)}, bf16[64,16,256]{2,1,0:T(8,128)(2,1)S(1)}, u32[]{:S(2)}) copy-start(bf16[64,16,256]{2,1,0:T(8,128)(2,1)S(1)} %pick.3) | copy-start | bytes 1572868
  61.3 14.5 %collective-permute-start.12 = (bf16[1024,256]{1,0:T(8,128)(2,1)S(1)}, bf16[1024,256]{1,0:T(8,128)(2,1)S(1)}, u32[]{:S(2)}, u32[]{:S(2)}) collective-permute-start(bf16[1024,256]{1,0:T(8,128)(2,1)S(1)} %bitcast.15), channel_id=1, source_target_pairs={{0,3},{1,0},{2,1},{3,2},{4,7},{5,4},{6,5},{7,6},{8,11},{9,8},{10,9... | collective-permute-start | bytes 1572872 | tf_op jit(solution)/shard_map/ppermute | solution.py:407
  64.0 15.3 %collective-permute-start.10 = (bf16[1024,256]{1,0:T(8,128)(2,1)S(1)}, bf16[1024,256]{1,0:T(8,128)(2,1)S(1)}, u32[]{:S(2)}, u32[]{:S(2)}) collective-permute-start(bf16[1024,256]{1,0:T(8,128)(2,1)S(1)} %bitcast.16), channel_id=1, source_target_pairs={{0,1},{1,2},{2,3},{3,0},{4,5},{5,6},{6,7},{7,4},{8,9},{9,10},{10,1... | collective-permute-start | bytes 1572872 | tf_op jit(solution)/shard_map/ppermute | solution.py:407
  64.5 7.3 %copy-start.12 = (bf16[512,256]{1,0:T(8,128)(2,1)}, bf16[512,256]{1,0:T(8,128)(2,1)S(1)}, u32[]{:S(2)}) copy-start(bf16[512,256]{1,0:T(8,128)(2,1)S(1)} %collective-permute-done.3.refs_3_) | copy-start | bytes 786436
  67.7 4.1 %copy-start.13 = (bf16[512,256]{1,0:T(8,128)(2,1)}, bf16[512,256]{1,0:T(8,128)(2,1)S(1)}, u32[]{:S(2)}) copy-start(bf16[512,256]{1,0:T(8,128)(2,1)S(1)} %collective-permute-done.1.refs_2_) | copy-start | bytes 786436
  71.8 1.0 copy-start.19
  72.8 8.6 %collective-permute-start.5 = (bf16[512,256]{1,0:T(8,128)(2,1)S(1)}, bf16[512,256]{1,0:T(8,128)(2,1)S(1)}, u32[]{:S(2)}, u32[]{:S(2)}) collective-permute-start(bf16[512,256]{1,0:T(8,128)(2,1)S(1)} %get-tuple-element.44), channel_id=1, source_target_pairs={{0,3},{1,0},{2,1},{3,2},{4,7},{5,4},{6,5},{7,6},{8,11},{9,8},{10,9... | collective-permute-start | bytes 786440 | tf_op jit(solution)/shard_map/ppermute | solution.py:407
  72.8 12.1 %collective-permute-start.8 = (bf16[512,256]{1,0:T(8,128)(2,1)S(1)}, bf16[512,256]{1,0:T(8,128)(2,1)S(1)}, u32[]{:S(2)}, u32[]{:S(2)}) collective-permute-start(bf16[512,256]{1,0:T(8,128)(2,1)S(1)} %get-tuple-element.48), channel_id=1, source_target_pairs={{0,1},{1,2},{2,3},{3,0},{4,5},{5,6},{6,7},{7,4},{8,9},{9,10},{10,1... | collective-permute-start | bytes 786440 | tf_op jit(solution)/shard_map/ppermute | solution.py:407
  75.8 18.2 %copy-start.5 = (bf16[1024,256]{1,0:T(8,128)(2,1)}, bf16[1024,256]{1,0:T(8,128)(2,1)S(1)}, u32[]{:S(2)}) copy-start(bf16[1024,256]{1,0:T(8,128)(2,1)S(1)} %collective-permute-done.12.refs_4_.refs_9_) | copy-start | bytes 1572868
  75.8 11.2 %collective-permute-start.13 = (bf16[512,256]{1,0:T(8,128)(2,1)S(1)}, bf16[512,256]{1,0:T(8,128)(2,1)S(1)}, u32[]{:S(2)}, u32[]{:S(2)}) collective-permute-start(bf16[512,256]{1,0:T(8,128)(2,1)S(1)} %slice.19), channel_id=1, source_target_pairs={{0,3},{1,0},{2,1},{3,2},{4,7},{5,4},{6,5},{7,6},{8,11},{9,8},{10,9... | collective-permute-start | bytes 786440 | tf_op jit(solution)/shard_map/ppermute | solution.py:407
  79.3 14.7 %copy-start.6 = (bf16[1024,256]{1,0:T(8,128)(2,1)}, bf16[1024,256]{1,0:T(8,128)(2,1)S(1)}, u32[]{:S(2)}) copy-start(bf16[1024,256]{1,0:T(8,128)(2,1)S(1)} %collective-permute-done.10.refs_1_.refs_6_) | copy-start | bytes 1572868
  79.3 10.8 %collective-permute-start.11 = (bf16[512,256]{1,0:T(8,128)(2,1)S(1)}, bf16[512,256]{1,0:T(8,128)(2,1)S(1)}, u32[]{:S(2)}, u32[]{:S(2)}) collective-permute-start(bf16[512,256]{1,0:T(8,128)(2,1)S(1)} %slice.18), channel_id=1, source_target_pairs={{0,1},{1,2},{2,3},{3,0},{4,5},{5,6},{6,7},{7,4},{8,9},{9,10},{10,1... | collective-permute-start | bytes 786440 | tf_op jit(solution)/shard_map/ppermute | solution.py:407
  79.6 16.2 %collective-permute-start.4 = (bf16[512,256]{1,0:T(8,128)(2,1)S(1)}, bf16[512,256]{1,0:T(8,128)(2,1)S(1)}, u32[]{:S(2)}, u32[]{:S(2)}) collective-permute-start(bf16[512,256]{1,0:T(8,128)(2,1)S(1)} %get-tuple-element.42), channel_id=1, source_target_pairs={{0,1},{1,2},{2,3},{3,0},{4,5},{5,6},{6,7},{7,4},{8,9},{9,10},{10,1... | collective-permute-start | bytes 786440 | tf_op jit(solution)/shard_map/ppermute | solution.py:407
  81.4 14.4 %collective-permute-start.7 = (bf16[512,256]{1,0:T(8,128)(2,1)S(1)}, bf16[512,256]{1,0:T(8,128)(2,1)S(1)}, u32[]{:S(2)}, u32[]{:S(2)}) collective-permute-start(bf16[512,256]{1,0:T(8,128)(2,1)S(1)} %get-tuple-element.46), channel_id=1, source_target_pairs={{0,3},{1,0},{2,1},{3,2},{4,7},{5,4},{6,5},{7,6},{8,11},{9,8},{10,9... | collective-permute-start | bytes 786440 | tf_op jit(solution)/shard_map/ppermute | solution.py:407
  84.9 13.4 %collective-permute-start.6 = (bf16[512,256]{1,0:T(8,128)(2,1)S(1)}, bf16[512,256]{1,0:T(8,128)(2,1)S(1)}, u32[]{:S(2)}, u32[]{:S(2)}) collective-permute-start(bf16[512,256]{1,0:T(8,128)(2,1)S(1)} %add_convert_fusion.3), channel_id=1, source_target_pairs={{0,3},{1,0},{2,1},{3,2},{4,7},{5,4},{6,5},{7,6},{8,11},{9,8},{10,9... | collective-permute-start | bytes 786440 | tf_op jit(solution)/shard_map/ppermute | solution.py:407
  87.0 7.0 %copy-start.14 = (bf16[512,256]{1,0:T(8,128)(2,1)}, bf16[512,256]{1,0:T(8,128)(2,1)S(1)}, u32[]{:S(2)}) copy-start(bf16[512,256]{1,0:T(8,128)(2,1)S(1)} %collective-permute-done.13.refs_3_.refs_8_) | copy-start | bytes 786436
  87.0 14.4 %collective-permute-start.9 = (bf16[512,256]{1,0:T(8,128)(2,1)S(1)}, bf16[512,256]{1,0:T(8,128)(2,1)S(1)}, u32[]{:S(2)}, u32[]{:S(2)}) collective-permute-start(bf16[512,256]{1,0:T(8,128)(2,1)S(1)} %add_convert_fusion.2), channel_id=1, source_target_pairs={{0,1},{1,2},{2,3},{3,0},{4,5},{5,6},{6,7},{7,4},{8,9},{9,10},{10,1... | collective-permute-start | bytes 786440 | tf_op jit(solution)/shard_map/ppermute | solution.py:407
  90.2 3.9 %copy-start.15 = (bf16[512,256]{1,0:T(8,128)(2,1)}, bf16[512,256]{1,0:T(8,128)(2,1)S(1)}, u32[]{:S(2)}) copy-start(bf16[512,256]{1,0:T(8,128)(2,1)S(1)} %collective-permute-done.11.refs_2_.refs_7_) | copy-start | bytes 786436
  94.1 1.0 copy-start.18
  95.0 7.4 %copy-start.16 = (bf16[512,256]{1,0:T(8,128)(2,1)}, bf16[512,256]{1,0:T(8,128)(2,1)S(1)}, u32[]{:S(2)}) copy-start(bf16[512,256]{1,0:T(8,128)(2,1)S(1)} %get-tuple-element.56) | copy-start | bytes 786436
  95.0 7.4 %copy-start.17 = (bf16[1024,512]{1,0:T(8,128)(2,1)}, bf16[1024,512]{1,0:T(8,128)(2,1)S(1)}, u32[]{:S(2)}) copy-start(bf16[1024,512]{1,0:T(8,128)(2,1)S(1)} %get-tuple-element.65.refs_11_) | copy-start | bytes 3145732
  102.5 31.2 %all-to-all-start.1 = ((bf16[64,16,256]{2,1,0:T(8,128)(2,1)}), bf16[64,16,256]{2,1,0:T(8,128)(2,1)S(1)}, u32[]{:S(2)}, u32[]{:S(2)}) async-start(bf16[64,16,256]{2,1,0:T(8,128)(2,1)} %bitcast.5), calls=%async_computation.1 | async-start | bytes 1048576 | tf_op jit(solution)/shard_map/all_to_all | solution.py:397
  112.7 7.7 %collective-permute-start.15 = (bf16[512,256]{1,0:T(8,128)(2,1)}, bf16[512,256]{1,0:T(8,128)(2,1)S(1)}, u32[]{:S(2)}, u32[]{:S(2)}) collective-permute-start(bf16[512,256]{1,0:T(8,128)(2,1)} %copy-done.16), channel_id=1, source_target_pairs={{0,3},{1,0},{2,1},{3,2},{4,7},{5,4},{6,5},{7,6},{8,11},{9,8},{10,9... | collective-permute-start | bytes 786440 | tf_op jit(solution)/shard_map/ppermute | solution.py:407
  112.8 9.1 %collective-permute-start.18 = (bf16[512,256]{1,0:T(8,128)(2,1)S(1)}, bf16[512,256]{1,0:T(8,128)(2,1)S(1)}, u32[]{:S(2)}, u32[]{:S(2)}) collective-permute-start(bf16[512,256]{1,0:T(8,128)(2,1)S(1)} %get-tuple-element.60), channel_id=1, source_target_pairs={{0,1},{1,2},{2,3},{3,0},{4,5},{5,6},{6,7},{7,4},{8,9},{9,10},{10,1... | collective-permute-start | bytes 786440 | tf_op jit(solution)/shard_map/ppermute | solution.py:407
  114.2 12.8 %collective-permute-start.14 = (bf16[512,256]{1,0:T(8,128)(2,1)S(1)}, bf16[512,256]{1,0:T(8,128)(2,1)S(1)}, u32[]{:S(2)}, u32[]{:S(2)}) collective-permute-start(bf16[512,256]{1,0:T(8,128)(2,1)S(1)} %get-tuple-element.54), channel_id=1, source_target_pairs={{0,1},{1,2},{2,3},{3,0},{4,5},{5,6},{6,7},{7,4},{8,9},{9,10},{10,1... | collective-permute-start | bytes 786440 | tf_op jit(solution)/shard_map/ppermute | solution.py:407
  114.2 12.7 %collective-permute-start.17 = (bf16[512,256]{1,0:T(8,128)(2,1)S(1)}, bf16[512,256]{1,0:T(8,128)(2,1)S(1)}, u32[]{:S(2)}, u32[]{:S(2)}) collective-permute-start(bf16[512,256]{1,0:T(8,128)(2,1)S(1)} %get-tuple-element.58), channel_id=1, source_target_pairs={{0,3},{1,0},{2,1},{3,2},{4,7},{5,4},{6,5},{7,6},{8,11},{9,8},{10,9... | collective-permute-start | bytes 786440 | tf_op jit(solution)/shard_map/ppermute | solution.py:407
  120.5 11.2 %collective-permute-start.16 = (bf16[512,256]{1,0:T(8,128)(2,1)S(1)}, bf16[512,256]{1,0:T(8,128)(2,1)S(1)}, u32[]{:S(2)}, u32[]{:S(2)}) collective-permute-start(bf16[512,256]{1,0:T(8,128)(2,1)S(1)} %add_convert_fusion.1), channel_id=1, source_target_pairs={{0,3},{1,0},{2,1},{3,2},{4,7},{5,4},{6,5},{7,6},{8,11},{9,8},{10,9... | collective-permute-start | bytes 786440 | tf_op jit(solution)/shard_map/ppermute | solution.py:407
  121.9 10.7 %collective-permute-start.19 = (bf16[512,256]{1,0:T(8,128)(2,1)S(1)}, bf16[512,256]{1,0:T(8,128)(2,1)S(1)}, u32[]{:S(2)}, u32[]{:S(2)}) collective-permute-start(bf16[512,256]{1,0:T(8,128)(2,1)S(1)} %add_convert_fusion), channel_id=1, source_target_pairs={{0,1},{1,2},{2,3},{3,0},{4,5},{5,6},{6,7},{7,4},{8,9},{9,10},{10,1... | collective-permute-start | bytes 786440 | tf_op jit(solution)/shard_map/ppermute | solution.py:407
  133.6 13.9 %copy-start.7 = (f32[8,128]{1,0:T(8,128)}, f32[8,128]{1,0:T(8,128)S(1)}, u32[]{:S(2)}) copy-start(f32[8,128]{1,0:T(8,128)S(1)} %get-tuple-element.61.refs_0_.refs_13_) | copy-start | bytes 12292
  133.6 29.1 %all-to-all-start.2 = ((bf16[64,16,256]{2,1,0:T(8,128)(2,1)}), bf16[64,16,256]{2,1,0:T(8,128)(2,1)S(1)}, u32[]{:S(2)}, u32[]{:S(2)}) async-start(bf16[64,16,256]{2,1,0:T(8,128)(2,1)} %bitcast.7), calls=%async_computation.2 | async-start | bytes 1048576 | tf_op jit(solution)/shard_map/all_to_all | solution.py:397
  145.5 11.7 %collective-permute-start.22 = (bf16[256,256]{1,0:T(8,128)(2,1)S(1)}, bf16[256,256]{1,0:T(8,128)(2,1)S(1)}, u32[]{:S(2)}, u32[]{:S(2)}) collective-permute-start(bf16[256,256]{1,0:T(8,128)(2,1)S(1)} %combine.2.refs_0_), channel_id=1, source_target_pairs={{0,3},{1,0},{2,1},{3,2},{4,7},{5,4},{6,5},{7,6},{8,11},{9,8},{10,9... | collective-permute-start | bytes 393224 | tf_op jit(solution)/shard_map/ppermute | solution.py:407
  145.7 11.5 %collective-permute-start.21 = (bf16[256,256]{1,0:T(8,128)(2,1)S(1)}, bf16[256,256]{1,0:T(8,128)(2,1)S(1)}, u32[]{:S(2)}, u32[]{:S(2)}) collective-permute-start(bf16[256,256]{1,0:T(8,128)(2,1)S(1)} %combine.2.refs_0_), channel_id=1, source_target_pairs={{0,2},{1,3},{2,0},{3,1},{4,6},{5,7},{6,4},{7,5},{8,10},{9,11},{10,... | collective-permute-start | bytes 393224 | tf_op jit(solution)/shard_map/ppermute | solution.py:407
  147.5 9.7 %collective-permute-start.20 = (bf16[256,256]{1,0:T(8,128)(2,1)S(1)}, bf16[256,256]{1,0:T(8,128)(2,1)S(1)}, u32[]{:S(2)}, u32[]{:S(2)}) collective-permute-start(bf16[256,256]{1,0:T(8,128)(2,1)S(1)} %combine.2.refs_0_), channel_id=1, source_target_pairs={{0,1},{1,2},{2,3},{3,0},{4,5},{5,6},{6,7},{7,4},{8,9},{9,10},{10,1... | collective-permute-start | bytes 393224 | tf_op jit(solution)/shard_map/ppermute | solution.py:407
  162.7 0.7 copy-start.8
  163.9 4.8 %collective-permute-start.25 = (bf16[256,256]{1,0:T(8,128)(2,1)S(1)}, bf16[256,256]{1,0:T(8,128)(2,1)S(1)}, u32[]{:S(2)}, u32[]{:S(2)}) collective-permute-start(bf16[256,256]{1,0:T(8,128)(2,1)S(1)} %combine.3.refs_0_), channel_id=1, source_target_pairs={{0,3},{1,0},{2,1},{3,2},{4,7},{5,4},{6,5},{7,6},{8,11},{9,8},{10,9... | collective-permute-start | bytes 393224 | tf_op jit(solution)/shard_map/ppermute | solution.py:407
  164.1 5.9 %collective-permute-start.24 = (bf16[256,256]{1,0:T(8,128)(2,1)S(1)}, bf16[256,256]{1,0:T(8,128)(2,1)S(1)}, u32[]{:S(2)}, u32[]{:S(2)}) collective-permute-start(bf16[256,256]{1,0:T(8,128)(2,1)S(1)} %combine.3.refs_0_), channel_id=1, source_target_pairs={{0,2},{1,3},{2,0},{3,1},{4,6},{5,7},{6,4},{7,5},{8,10},{9,11},{10,... | collective-permute-start | bytes 393224 | tf_op jit(solution)/shard_map/ppermute | solution.py:407
  165.9 7.4 %collective-permute-start.23 = (bf16[256,256]{1,0:T(8,128)(2,1)S(1)}, bf16[256,256]{1,0:T(8,128)(2,1)S(1)}, u32[]{:S(2)}, u32[]{:S(2)}) collective-permute-start(bf16[256,256]{1,0:T(8,128)(2,1)S(1)} %combine.3.refs_0_), channel_id=1, source_target_pairs={{0,1},{1,2},{2,3},{3,0},{4,5},{5,6},{6,7},{7,4},{8,9},{9,10},{10,1... | collective-permute-start | bytes 393224 | tf_op jit(solution)/shard_map/ppermute | solution.py:407
where the time goes:
time: 175 us
  waiting for transfers between devices  54.2 us (31%)
  starting transfers between devices  49.3 us (28%)
  blocking collectives  41.1 us (23%)
  Pallas kernels  26 us (15%)
  local copies, waits for them, and re-layouts  2.81 us (2%)
    ppermute x26, waiting for transfers between devices, shift_by(): lax.ppermute(values, 'tensor', [(i, (i + step) % size) for i in range(siz...  49.5 us
    all_to_all x1, blocking collectives, swap_blocks(): lax.all_to_all(values, 'expert', split_axis=0, concat_axis=0, tiled=True)  41.1 us
    ppermute x26, starting transfers between devices, shift_by(): lax.ppermute(values, 'tensor', [(i, (i + step) % size) for i in range(siz...  27.8 us
    all_to_all x2, starting transfers between devices, swap_blocks(): lax.all_to_all(values, 'expert', split_axis=0, concat_axis=0, tiled=True)  21.5 us
    pallas_call x1, Pallas kernels, weight_grads(): pl.pallas_call(functools.partial(weights_kernel, parts, counts), in_specs...  9.64 us
    all_to_all x2, waiting for transfers between devices, swap_blocks(): lax.all_to_all(values, 'expert', split_axis=0, concat_axis=0, tiled=True)  4.67 us
    pallas_call x1, Pallas kernels, forward(): pl.pallas_call(functools.partial(forward_kernel, parts, halves, counts),...  4.02 us
    pallas_call x1, Pallas kernels, backward(): pl.pallas_call(functools.partial(backward_kernel, parts, halves, counts),...  3.84 us
  transfers between devices with their start and end apart: 28, of which 18 were waited for; matrix products, arithmetic and copies ran while one was open for 0% of the time, Pallas kernels for 11%

commit v1 on v0

--- a/solution.py
+++ b/solution.py
@@ -23,6 +23,7 @@
 ANY = pl.BlockSpec(memory_space=pl.ANY)
 HBM = pl.BlockSpec(memory_space=pltpu.HBM)
 TOKEN = jax.ShapeDtypeStruct((8, 128), F32)
+MARK = jax.ShapeDtypeStruct((1,), jnp.int32)
 
 
 def one_hot(place, height):
@@ -30,7 +31,7 @@
     return (lines == place).astype(F32).astype(BF16)
 
 
-def dispatch_kernel(capacity, experts, me, routes_in, mix_in, tokens_in, cotangent_in, sent, info, *scratch):
+def dispatch_kernel(capacity, experts, me, routes_in, mix_in, tokens_in, cotangent_in, x_out, g_out, info, *scratch):
     routes, mix, tokens, cotangent, sems = scratch
     rows, width = tokens.shape
     mine = pl.ds(pl.multiple_of(me[0] * width, width), width)
@@ -66,12 +67,12 @@
     ).T
     info[...] = columns
     x = dot(pick0 + pick1, tokens[...], NN).astype(BF16)
-    sent[:, pl.ds(0, capacity), :] = x.reshape(experts, capacity, x.shape[1])
+    x_out[...] = x.reshape(x_out.shape)
     cot = cotangent[...].astype(F32)
     scaled0 = (columns[:, 2:3] * cot).astype(BF16)
     scaled1 = (columns[:, 3:4] * cot).astype(BF16)
     g = (dot(pick0, scaled0, NN) + dot(pick1, scaled1, NN)).astype(BF16)
-    sent[:, pl.ds(capacity, capacity), :] = g.reshape(experts, capacity, g.shape[1])
+    g_out[...] = g.reshape(g_out.shape)
 
 
 def dispatch(me, routes, mix, tokens, cotangent, experts, capacity, parts):
@@ -79,9 +80,10 @@
     return pl.pallas_call(
         functools.partial(dispatch_kernel, capacity, experts),
         in_specs=[SMEM] + [HBM] * 4,
-        out_specs=[VMEM] * 2,
+        out_specs=[VMEM] * 3,
         out_shape=(
-            jax.ShapeDtypeStruct((experts, 2 * capacity, width), BF16),
+            jax.ShapeDtypeStruct((experts, capacity, width), BF16),
+            jax.ShapeDtypeStruct((experts, capacity, width), BF16),
             jax.ShapeDtypeStruct((rows, 8), F32),
         ),
         scratch_shapes=[
@@ -96,25 +98,31 @@
     )(me, routes.T, mix.T, tokens, cotangent)
 
 
-def pick_kernel(start, received, after, out):
-    out[...] = received[:, pl.ds(start, out.shape[1]), :]
-
-
-def pick(received, start, capacity, after):
-    experts, _, width = received.shape
-    return pl.pallas_call(
-        functools.partial(pick_kernel, start),
-        in_specs=[VMEM, VMEM],
-        out_specs=VMEM,
-        out_shape=jax.ShapeDtypeStruct((experts, capacity, width), BF16),
-        compiler_params=pltpu.CompilerParams(vmem_limit_bytes=2 << 20),
-        name="pick",
-    )(received, after).reshape(experts * capacity, width)
-
-
 def column_block(me, shift, parts, width):
     owner = lax.rem(me[0] + (parts - shift), parts)
     return pl.multiple_of(owner * width, width)
+
+
+def load_kernel(after, *refs):
+    count = (len(refs) - 1) // 2
+    sources, slots, sems = refs[:count], refs[count : 2 * count], refs[-1]
+    copies = [pltpu.make_async_copy(source, slot, sems.at[i]) for i, (source, slot) in enumerate(zip(sources, slots))]
+    for copy in copies:
+        copy.start()
+    for copy in copies:
+        copy.wait()
+
+
+def load(arrays, after):
+    return pl.pallas_call(
+        load_kernel,
+        in_specs=[VMEM] + [HBM] * len(arrays),
+        out_specs=[VMEM] * len(arrays),
+        out_shape=[jax.ShapeDtypeStruct(v.shape, v.dtype) for v in arrays],
+        scratch_shapes=[pltpu.SemaphoreType.DMA((len(arrays),))],
+        compiler_params=pltpu.CompilerParams(vmem_limit_bytes=50 << 20),
+        name="load",
+    )(after, *arrays)
 
 
 def by_chunk(refs, counts, halves):
@@ -230,7 +238,7 @@
     grad_gate, grad_up, grad_down, done = refs[2 * n + 4 : 2 * n + 8]
     x, g, units_in, tall, wide, in_sems, out_sems = refs[2 * n + 8 :]
     rows, width = x.shape[1:]
-    done[...] = jnp.zeros(done.shape, F32)
+    done[0] = 0
 
     def fetch(kind, shift):
         first = kind * n + sum(counts[:shift])
@@ -289,12 +297,12 @@
     return pl.pallas_call(
         functools.partial(weights_kernel, parts, counts),
         in_specs=[SMEM] + [HBM] * (2 * n + 3) + [VMEM],
-        out_specs=[HBM] * 3 + [VMEM],
+        out_specs=[HBM] * 3 + [SMEM],
         out_shape=(
             jax.ShapeDtypeStruct((1, parts * width, units), F32),
             jax.ShapeDtypeStruct((1, parts * width, units), F32),
             jax.ShapeDtypeStruct((1, units, parts * width), F32),
-            TOKEN,
+            MARK,
         ),
         scratch_shapes=[
             pltpu.VMEM((parts, rows, width), BF16),
@@ -314,9 +322,10 @@
 
 
 def total_kernel(halves, *refs):
-    out, done = refs[-2:]
-    terms = len(refs[:-3]) // halves
+    out, done, mark = refs[-3:]
+    terms = len(refs[:-4]) // halves
     done[...] = jnp.zeros(done.shape, F32)
+    mark[0] = 0
     rows = refs[0].shape[0]
     step = 32
 
@@ -335,8 +344,8 @@
     return pl.pallas_call(
         functools.partial(total_kernel, len(groups)),
         in_specs=[VMEM] * sum(map(len, groups)) + [VMEM],
-        out_specs=[VMEM] * 2,
-        out_shape=(jax.ShapeDtypeStruct((len(groups) * rows, width), BF16), TOKEN),
+        out_specs=[VMEM] * 2 + [SMEM],
+        out_shape=(jax.ShapeDtypeStruct((len(groups) * rows, width), BF16), TOKEN, MARK),
         compiler_params=pltpu.CompilerParams(vmem_limit_bytes=2 << 20),
         name="totals",
     )(*[v for group in groups for v in group], after)
@@ -344,7 +353,7 @@
 
 def assemble_kernel(parts, me, *refs):
     out, done, sems = refs[parts:]
-    done[...] = jnp.zeros(done.shape, F32)
+    done[0] = 0
     width = refs[0].shape[1]
     copies = []
     for shift in range(parts):
@@ -361,8 +370,8 @@
     return pl.pallas_call(
         functools.partial(assemble_kernel, parts),
         in_specs=[SMEM] + [VMEM] * parts,
-        out_specs=[HBM, VMEM],
-        out_shape=(jax.ShapeDtypeStruct((rows, width * parts), BF16), TOKEN),
+        out_specs=[HBM, SMEM],
+        out_shape=(jax.ShapeDtypeStruct((rows, width * parts), BF16), MARK),
         scratch_shapes=[pltpu.SemaphoreType.DMA((parts,))],
         compiler_params=pltpu.CompilerParams(vmem_limit_bytes=2 << 20),
         name="assemble",
@@ -385,7 +394,7 @@
 def combine(info, back, weighted, after):
     return pl.pallas_call(
         functools.partial(combine_kernel, weighted),
-        in_specs=[VMEM] * (2 + len(after)),
+        in_specs=[VMEM] * 2 + [SMEM] * len(after),
         out_specs=VMEM,
         out_shape=jax.ShapeDtypeStruct((info.shape[0], back.shape[1]), BF16),
         compiler_params=pltpu.CompilerParams(vmem_limit_bytes=8 << 20),
@@ -446,19 +455,21 @@
     parts = lax.axis_size("tensor")
     capacity = 4 * tokens.shape[0] // experts
     me = lax.axis_index("tensor").astype(jnp.int32).reshape(1)
-    sent, info = dispatch(me, routes, mix_weights, tokens, cotangent, experts, capacity, parts)
-    received = swap_blocks(sent)
-    x = gather_ring(pick(received, 0, capacity, info))
-    g = gather_ring(pick(received, capacity, capacity, info))
+    x_sent, g_sent, info = dispatch(me, routes, mix_weights, tokens, cotangent, experts, capacity, parts)
+    rows = experts * capacity
+    x = gather_ring(swap_blocks(x_sent).reshape(rows, x_sent.shape[2]))
+    g_mine = swap_blocks(g_sent).reshape(rows, g_sent.shape[2])
+    g = gather_ring(g_mine)
+    w_gate, w_up, w_down = load((w_gate, w_up, w_down), g_mine)
     pre_gate, pre_up, hidden, partial_out = forward(me, x, w_gate, w_up, w_down)
     out_terms = scatter_ring(partial_out)
     d_gate, d_up, after_backward, partial_in = backward(me, g, pre_gate, pre_up, w_gate, w_up, w_down)
-    out_mine, _ = totals(out_terms, after_backward)
+    out_mine, _, _ = totals(out_terms, after_backward)
     out_back = send_back(out_mine, experts, capacity)
-    in_mine, after_sums = totals(scatter_ring(partial_in), after_backward)
+    in_mine, after_sums, summed = totals(scatter_ring(partial_in), after_backward)
     in_back = send_back(in_mine, experts, capacity)
     grad_gate, grad_up, grad_down, after_weights = weight_grads(me, x, g, hidden, d_gate, d_up, after_sums)
-    result, after_result = gather_columns(me, combine(info, out_back, True, [after_sums]))
+    result, after_result = gather_columns(me, combine(info, out_back, True, [summed]))
     grad_tokens, _ = gather_columns(me, combine(info, in_back, False, [after_weights, after_result]))
     return (result, grad_tokens, grad_gate, grad_up, grad_down)
 

time: 175 us -> 176 us (level)
  blocking collectives: 41.1 us -> 30.7 us
  starting transfers between devices: 49.3 us -> 57.6 us
  Pallas kernels: 26 us -> 29.7 us
    all_to_all x1, blocking collectives: 41.1 us -> 30.7 us  [swap_blocks(): lax.all_to_all(values, 'expert', split_axis=0, concat_axis=0, tiled=True)]
    all_to_all x2 -> x3, starting transfers between devices: 21.5 us -> 29.6 us  [swap_blocks(): lax.all_to_all(values, 'expert', split_axis=0, concat_axis=0, tiled=True)]
    pallas_call x2, Pallas kernels: 1 us -> 2.86 us  [combine(): pl.pallas_call(functools.partial(combine_kernel, weighted), in_specs=[VME...]
    pallas_call x2 -> x1, Pallas kernels: 0.07 us -> 1.88 us  [load(): pl.pallas_call(load_kernel, in_specs=[VMEM] + [HBM] * len(arrays), out_sp...]
    all_to_all x2 -> x3, waiting for transfers between devices: 4.67 us -> 3.99 us  [swap_blocks(): lax.all_to_all(values, 'expert', split_axis=0, concat_axis=0, tiled=True)]
  transfers between devices with their start and end apart: 28 -> 29, of which waited for: 18 -> 18; matrix products, arithmetic and copies ran while one was open for 0% -> 0% of each run, Pallas kernels for 11% -> 13%
where the time goes in v1:
time: 176 us
  starting transfers between devices  57.6 us (33%)
  waiting for transfers between devices  53.5 us (30%)
  blocking collectives  30.7 us (17%)
  Pallas kernels  29.7 us (17%)
  local copies, waits for them, and re-layouts  2.69 us (2%)
    ppermute x26, waiting for transfers between devices, shift_by(): lax.ppermute(values, 'tensor', [(i, (i + step) % size) for i in range(siz...  49.5 us
    all_to_all x1, blocking collectives, swap_blocks(): lax.all_to_all(values, 'expert', split_axis=0, concat_axis=0, tiled=True)  30.7 us
    all_to_all x3, starting transfers between devices, swap_blocks(): lax.all_to_all(values, 'expert', split_axis=0, concat_axis=0, tiled=True)  29.6 us
    ppermute x26, starting transfers between devices, shift_by(): lax.ppermute(values, 'tensor', [(i, (i + step) % size) for i in range(siz...  28 us
    pallas_call x1, Pallas kernels, weight_grads(): pl.pallas_call(functools.partial(weights_kernel, parts, counts), in_specs...  9.57 us
    all_to_all x3, waiting for transfers between devices, swap_blocks(): lax.all_to_all(values, 'expert', split_axis=0, concat_axis=0, tiled=True)  3.99 us
    pallas_call x1, Pallas kernels, forward(): pl.pallas_call(functools.partial(forward_kernel, parts, halves, counts),...  3.96 us
    pallas_call x1, Pallas kernels, backward(): pl.pallas_call(functools.partial(backward_kernel, parts, halves, counts),...  3.66 us
  transfers between devices with their start and end apart: 29, of which 18 were waited for; matrix products, arithmetic and copies ran while one was open for 0% of the time, Pallas kernels for 13%

profile of v1, /device:TPU:1, one launch (start us, length us, event | category | flops | bytes accessed | tf_op | source)
XLA Modules:
  0.0 175.7 jit_solution(5291932642891976736)
XLA Ops:
  0.6 3.0 %dispatch.1 = (bf16[64,16,256]{2,1,0:T(8,128)(2,1)}, bf16[64,16,256]{2,1,0:T(8,128)(2,1)}, f32[256,8]{1,0:T(8,128)}) custom-call(s32[1]{0:T(128)} %bitcast.me, s32[2,256]{1,0:T(2,128)} %bitcast.20, f32[2,256]{1,0:T(2,128)} %bitcast.21, bf16[256,1024]{1,0:T(8,128)(2,1)} %tokens_in.1, bf16[256,1024]{1,0:T(8,128)(2,1)} %cotangent_in.1), custom_call_target="tpu_custom_call" | custom-call | tf_op jit(solution)/shard_map/dispatch/pallas_call | solution.py:80
  3.6 30.7 %all_to_all.20 = bf16[64,16,256]{2,1,0:T(8,128)(2,1)S(1)} all-to-all(bf16[64,16,256]{2,1,0:T(8,128)(2,1)} %get-tuple-element.45), channel_id=1, replica_groups=mesh['expert'=64,'tensor'=4] {'expert'}, dimensions={0} | all-to-all | bytes 1048576 | tf_op jit(solution)/shard_map/all_to_all | solution.py:406
  34.3 5.7 %all-to-all-start.1 = ((bf16[64,16,256]{2,1,0:T(8,128)(2,1)}), bf16[64,16,256]{2,1,0:T(8,128)(2,1)S(1)}, u32[]{:S(2)}, u32[]{:S(2)}) async-start(bf16[64,16,256]{2,1,0:T(8,128)(2,1)} %get-tuple-element.46), calls=%async_computation.1 | async-start | bytes 1048576 | tf_op jit(solution)/shard_map/all_to_all | solution.py:406
  40.1 2.8 %collective-permute-start.2 = (bf16[1024,256]{1,0:T(8,128)(2,1)S(1)}, bf16[1024,256]{1,0:T(8,128)(2,1)S(1)}, u32[]{:S(2)}, u32[]{:S(2)}) collective-permute-start(bf16[1024,256]{1,0:T(8,128)(2,1)S(1)} %bitcast.16), channel_id=1, source_target_pairs={{0,3},{1,0},{2,1},{3,2},{4,7},{5,4},{6,5},{7,6},{8,11},{9,8},{10,9... | collective-permute-start | bytes 1572872 | tf_op jit(solution)/shard_map/ppermute | solution.py:416
  42.9 10.8 %collective-permute-done.2.refs_4_ = bf16[1024,256]{1,0:T(8,128)(2,1)S(1)} collective-permute-done((bf16[1024,256]{1,0:T(8,128)(2,1)S(1)}, bf16[1024,256]{1,0:T(8,128)(2,1)S(1)}, u32[]{:S(2)}, u32[]{:S(2)}) %collective-permute-start.2) | collective-permute-done | bytes 524320 | tf_op jit(solution)/shard_map/ppermute | solution.py:416
  53.7 3.5 %collective-permute-start.3 = (bf16[512,256]{1,0:T(8,128)(2,1)S(1)}, bf16[512,256]{1,0:T(8,128)(2,1)S(1)}, u32[]{:S(2)}, u32[]{:S(2)}) collective-permute-start(bf16[512,256]{1,0:T(8,128)(2,1)S(1)} %slice.17), channel_id=1, source_target_pairs={{0,3},{1,0},{2,1},{3,2},{4,7},{5,4},{6,5},{7,6},{8,11},{9,8},{10,9... | collective-permute-start | bytes 786440 | tf_op jit(solution)/shard_map/ppermute | solution.py:416
  57.3 0.1 collective-permute-start.1
  57.3 0.4 all-to-all-done.1
  57.8 2.7 %collective-permute-start.12 = (bf16[1024,256]{1,0:T(8,128)(2,1)S(1)}, bf16[1024,256]{1,0:T(8,128)(2,1)S(1)}, u32[]{:S(2)}, u32[]{:S(2)}) collective-permute-start(bf16[1024,256]{1,0:T(8,128)(2,1)S(1)} %bitcast.9), channel_id=1, source_target_pairs={{0,3},{1,0},{2,1},{3,2},{4,7},{5,4},{6,5},{7,6},{8,11},{9,8},{10,9... | collective-permute-start | bytes 1572872 | tf_op jit(solution)/shard_map/ppermute | solution.py:416
  60.5 0.0 collective-permute-start.10
  60.5 1.9 %load.1 = (bf16[1,1024,512]{2,1,0:T(8,128)(2,1)S(1)}, bf16[1,1024,512]{2,1,0:T(8,128)(2,1)S(1)}, bf16[1,512,1024]{2,1,0:T(8,128)(2,1)S(1)}) custom-call(bf16[1024,256]{1,0:T(8,128)(2,1)S(1)} %bitcast.11, bf16[1,1024,512]{2,1,0:T(8,128)(2,1)} %refs_0_.1, bf16[1,1024,512]{2,1,0:T(8,128)(2,1)} %refs_1_.1, bf16[1,512,1024]{2,1,0:T(8,128)(2,1)} %refs_2_.1), custom_call_target="tpu_custom_call" | custom-call | tf_op jit(solution)/shard_map/load/pallas_call | solution.py:117
  62.4 0.0 collective-permute-done.3.refs_3_
  62.4 2.3 %collective-permute-done.1.refs_2_ = bf16[512,256]{1,0:T(8,128)(2,1)S(1)} collective-permute-done((bf16[512,256]{1,0:T(8,128)(2,1)S(1)}, bf16[512,256]{1,0:T(8,128)(2,1)S(1)}, u32[]{:S(2)}, u32[]{:S(2)}) %collective-permute-start.1) | collective-permute-done | bytes 262176 | tf_op jit(solution)/shard_map/ppermute | solution.py:416
  64.8 4.0 %forward.1 = (f32[1024,512]{1,0:T(8,128)S(1)}, f32[1024,512]{1,0:T(8,128)S(1)}, bf16[1024,512]{1,0:T(8,128)(2,1)S(1)}, bf16[512,256]{1,0:T(8,128)(2,1)S(1)}, bf1...) custom-call(s32[1]{0:T(128)} %bitcast.me, ...), custom_call_target="tpu_custom_call" | custom-call | flops 3221225472 | bytes 12582912 | tf_op jit(solution)/shard_map/forward/pallas_call | solution.py:170
  68.8 1.0 copy-done.16
  69.8 0.4 collective-permute-start.5
  70.2 1.1 collective-permute-start.8
  71.3 1.5 collective-permute-done.12.refs_4_.refs_9_
  72.8 3.7 %collective-permute-start.13 = (bf16[512,256]{1,0:T(8,128)(2,1)S(1)}, bf16[512,256]{1,0:T(8,128)(2,1)S(1)}, u32[]{:S(2)}, u32[]{:S(2)}) collective-permute-start(bf16[512,256]{1,0:T(8,128)(2,1)S(1)} %slice.19), channel_id=1, source_target_pairs={{0,3},{1,0},{2,1},{3,2},{4,7},{5,4},{6,5},{7,6},{8,11},{9,8},{10,9... | collective-permute-start | bytes 786440 | tf_op jit(solution)/shard_map/ppermute | solution.py:416
  76.5 0.0 collective-permute-done.10.refs_1_.refs_6_
  76.5 0.1 collective-permute-start.11
  76.6 0.1 collective-permute-start.4
  76.7 1.7 collective-permute-done.5
  78.4 3.4 %collective-permute-start.7 = (bf16[512,256]{1,0:T(8,128)(2,1)S(1)}, bf16[512,256]{1,0:T(8,128)(2,1)S(1)}, u32[]{:S(2)}, u32[]{:S(2)}) collective-permute-start(bf16[512,256]{1,0:T(8,128)(2,1)S(1)} %get-tuple-element.55), channel_id=1, source_target_pairs={{0,3},{1,0},{2,1},{3,2},{4,7},{5,4},{6,5},{7,6},{8,11},{9,8},{10,9... | collective-permute-start | bytes 786440 | tf_op jit(solution)/shard_map/ppermute | solution.py:416
  81.8 0.1 add_convert_fusion.3
  81.9 0.1 collective-permute-start.6
  82.0 0.1 add_convert_fusion.2
  82.0 2.0 %collective-permute-done.13.refs_3_.refs_8_ = bf16[512,256]{1,0:T(8,128)(2,1)S(1)} collective-permute-done((bf16[512,256]{1,0:T(8,128)(2,1)S(1)}, bf16[512,256]{1,0:T(8,128)(2,1)S(1)}, u32[]{:S(2)}, u32[]{:S(2)}) %collective-permute-start.13) | collective-permute-done | bytes 262176 | tf_op jit(solution)/shard_map/ppermute | solution.py:416
  84.0 3.2 %collective-permute-done.11.refs_2_.refs_7_ = bf16[512,256]{1,0:T(8,128)(2,1)S(1)} collective-permute-done((bf16[512,256]{1,0:T(8,128)(2,1)S(1)}, bf16[512,256]{1,0:T(8,128)(2,1)S(1)}, u32[]{:S(2)}, u32[]{:S(2)}) %collective-permute-start.11) | collective-permute-done | bytes 262176 | tf_op jit(solution)/shard_map/ppermute | solution.py:416
  87.2 3.7 %backward.1 = (bf16[1024,512]{1,0:T(8,128)(2,1)S(1)}, bf16[1024,512]{1,0:T(8,128)(2,1)S(1)}, f32[8,128]{1,0:T(8,128)S(1)}, bf16[512,256]{1,0:T(8,128)(2,1)S(1)},...) custom-call(s32[1]{0:T(128)} %bitcast.me, ...), custom_call_target="tpu_custom_call" | custom-call | flops 3221225472 | bytes 12582912 | tf_op jit(solution)/shard_map/backward/pallas_call | solution.py:219
  91.0 1.0 copy-done.15
  91.9 0.9 collective-permute-done.4.refs_1_
  92.9 2.4 %collective-permute-done.6.refs_2_ = bf16[512,256]{1,0:T(8,128)(2,1)S(1)} collective-permute-done((bf16[512,256]{1,0:T(8,128)(2,1)S(1)}, bf16[512,256]{1,0:T(8,128)(2,1)S(1)}, u32[]{:S(2)}, u32[]{:S(2)}) %collective-permute-start.6) | collective-permute-done | bytes 262176 | tf_op jit(solution)/shard_map/ppermute | solution.py:416
  95.2 3.2 %collective-permute-done.9.refs_5_ = bf16[512,256]{1,0:T(8,128)(2,1)S(1)} collective-permute-done((bf16[512,256]{1,0:T(8,128)(2,1)S(1)}, bf16[512,256]{1,0:T(8,128)(2,1)S(1)}, u32[]{:S(2)}, u32[]{:S(2)}) %collective-permute-start.9) | collective-permute-done | bytes 262176 | tf_op jit(solution)/shard_map/ppermute | solution.py:416
  98.5 1.1 totals.2
  99.6 12.5 %all-to-all-start.2 = ((bf16[64,16,256]{2,1,0:T(8,128)(2,1)}), bf16[64,16,256]{2,1,0:T(8,128)(2,1)S(1)}, u32[]{:S(2)}, u32[]{:S(2)}) async-start(bf16[64,16,256]{2,1,0:T(8,128)(2,1)} %bitcast.5), calls=%async_computation.2 | async-start | bytes 1048576 | tf_op jit(solution)/shard_map/all_to_all | solution.py:406
  112.1 0.1 collective-permute-start.15
  112.2 1.5 collective-permute-start.18
  113.7 0.0 collective-permute-start.14
  113.7 2.6 %collective-permute-start.17 = (bf16[512,256]{1,0:T(8,128)(2,1)S(1)}, bf16[512,256]{1,0:T(8,128)(2,1)S(1)}, u32[]{:S(2)}, u32[]{:S(2)}) collective-permute-start(bf16[512,256]{1,0:T(8,128)(2,1)S(1)} %get-tuple-element.67), channel_id=1, source_target_pairs={{0,3},{1,0},{2,1},{3,2},{4,7},{5,4},{6,5},{7,6},{8,11},{9,8},{10,9... | collective-permute-start | bytes 786440 | tf_op jit(solution)/shard_map/ppermute | solution.py:416
  116.4 3.5 %collective-permute-done.15 = bf16[512,256]{1,0:T(8,128)(2,1)S(1)} collective-permute-done((bf16[512,256]{1,0:T(8,128)(2,1)}, bf16[512,256]{1,0:T(8,128)(2,1)S(1)}, u32[]{:S(2)}, u32[]{:S(2)}) %collective-permute-start.15) | collective-permute-done | bytes 262176 | tf_op jit(solution)/shard_map/ppermute | solution.py:416
  119.9 0.1 add_convert_fusion.1
  119.9 1.4 collective-permute-start.16
  121.3 0.1 add_convert_fusion
  121.4 0.4 collective-permute-start.19
  121.8 4.8 %collective-permute-done.14.refs_1_ = bf16[512,256]{1,0:T(8,128)(2,1)S(1)} collective-permute-done((bf16[512,256]{1,0:T(8,128)(2,1)S(1)}, bf16[512,256]{1,0:T(8,128)(2,1)S(1)}, u32[]{:S(2)}, u32[]{:S(2)}) %collective-permute-start.14) | collective-permute-done | bytes 262176 | tf_op jit(solution)/shard_map/ppermute | solution.py:416
  126.7 4.4 %collective-permute-done.16.refs_2_ = bf16[512,256]{1,0:T(8,128)(2,1)S(1)} collective-permute-done((bf16[512,256]{1,0:T(8,128)(2,1)S(1)}, bf16[512,256]{1,0:T(8,128)(2,1)S(1)}, u32[]{:S(2)}, u32[]{:S(2)}) %collective-permute-start.16) | collective-permute-done | bytes 262176 | tf_op jit(solution)/shard_map/ppermute | solution.py:416
  131.1 1.2 collective-permute-done.19.refs_5_
  132.3 1.1 totals.3
  133.4 0.6 copy-done.13
  134.0 11.3 %all-to-all-start.3 = ((bf16[64,16,256]{2,1,0:T(8,128)(2,1)}), bf16[64,16,256]{2,1,0:T(8,128)(2,1)S(1)}, u32[]{:S(2)}, u32[]{:S(2)}) async-start(bf16[64,16,256]{2,1,0:T(8,128)(2,1)} %bitcast.7), calls=%async_computation.3 | async-start | bytes 1048576 | tf_op jit(solution)/shard_map/all_to_all | solution.py:406
  145.3 1.1 combine.2.refs_0_
  146.5 0.1 collective-permute-start.22
  146.6 1.9 %collective-permute-start.21 = (bf16[256,256]{1,0:T(8,128)(2,1)S(1)}, bf16[256,256]{1,0:T(8,128)(2,1)S(1)}, u32[]{:S(2)}, u32[]{:S(2)}) collective-permute-start(bf16[256,256]{1,0:T(8,128)(2,1)S(1)} %combine.2.refs_0_), channel_id=1, source_target_pairs={{0,2},{1,3},{2,0},{3,1},{4,6},{5,7},{6,4},{7,5},{8,10},{9,11},{10,... | collective-permute-start | bytes 393224 | tf_op jit(solution)/shard_map/ppermute | solution.py:416
  148.5 9.6 %weight_grads.1 = (f32[1,1024,512]{2,1,0:T(8,128)}, f32[1,1024,512]{2,1,0:T(8,128)}, f32[1,512,1024]{2,1,0:T(8,128)}, s32[1]{0:T(128)}) custom-call(s32[1]{0:T(128)} %bitcast.me, bf16[1024,256]{1,0:T(8,128)(2,1)} %bitcast.19, bf16[1024,256]{1,0:T(8,128)(2,1)} %copy-done.4, bf16[512,256]{1,0:T(8,128)(2,1)} %copy-done.8, bf16[512,256]{1,0:T(8,128)(2,1)} %copy-done.7, ...), custom_call_target="tpu_custom_call" | custom-call | flops 3221225472 | bytes 13631488 | tf_op jit(solution)/shard_map/weight_grads/pallas_call | solution.py:297
  158.1 1.3 assemble.2
  159.5 3.6 %all-to-all-done.3 = bf16[64,16,256]{2,1,0:T(8,128)(2,1)S(1)} async-done(((bf16[64,16,256]{2,1,0:T(8,128)(2,1)}), bf16[64,16,256]{2,1,0:T(8,128)(2,1)S(1)}, u32[]{:S(2)}, u32[]{:S(2)}) %all-to-all-start.3) | async-done | bytes 524320 | tf_op jit(solution)/shard_map/all_to_all | solution.py:406
  163.0 1.7 combine.3.refs_0_
  164.7 0.1 collective-permute-start.25
  164.8 1.9 %collective-permute-start.24 = (bf16[256,256]{1,0:T(8,128)(2,1)S(1)}, bf16[256,256]{1,0:T(8,128)(2,1)S(1)}, u32[]{:S(2)}, u32[]{:S(2)}) collective-permute-start(bf16[256,256]{1,0:T(8,128)(2,1)S(1)} %combine.3.refs_0_), channel_id=1, source_target_pairs={{0,2},{1,3},{2,0},{3,1},{4,6},{5,7},{6,4},{7,5},{8,10},{9,11},{10,... | collective-permute-start | bytes 393224 | tf_op jit(solution)/shard_map/ppermute | solution.py:416
  166.8 2.7 %collective-permute-done.25.refs_3_ = bf16[256,256]{1,0:T(8,128)(2,1)S(1)} collective-permute-done((bf16[256,256]{1,0:T(8,128)(2,1)S(1)}, bf16[256,256]{1,0:T(8,128)(2,1)S(1)}, u32[]{:S(2)}, u32[]{:S(2)}) %collective-permute-start.25) | collective-permute-done | bytes 131104 | tf_op jit(solution)/shard_map/ppermute | solution.py:416
  169.5 1.4 collective-permute-done.24.refs_2_
  170.9 3.3 %collective-permute-done.23.refs_1_ = bf16[256,256]{1,0:T(8,128)(2,1)S(1)} collective-permute-done((bf16[256,256]{1,0:T(8,128)(2,1)S(1)}, bf16[256,256]{1,0:T(8,128)(2,1)S(1)}, u32[]{:S(2)}, u32[]{:S(2)}) %collective-permute-start.23) | collective-permute-done | bytes 131104 | tf_op jit(solution)/shard_map/ppermute | solution.py:416
  174.2 1.3 assemble.3
  (48 shorter events, 0.2 us)
Async XLA Ops:
  34.3 30.4 %copy-start.1 = (bf16[64,16,256]{2,1,0:T(8,128)(2,1)}, bf16[64,16,256]{2,1,0:T(8,128)(2,1)S(1)}, u32[]{:S(2)}) copy-start(bf16[64,16,256]{2,1,0:T(8,128)(2,1)S(1)} %all_to_all.20) | copy-start | bytes 1572868
  34.3 23.4 %all-to-all-start.1 = ((bf16[64,16,256]{2,1,0:T(8,128)(2,1)}), bf16[64,16,256]{2,1,0:T(8,128)(2,1)S(1)}, u32[]{:S(2)}, u32[]{:S(2)}) async-start(bf16[64,16,256]{2,1,0:T(8,128)(2,1)} %get-tuple-element.46), calls=%async_computation.1 | async-start | bytes 1048576 | tf_op jit(solution)/shard_map/all_to_all | solution.py:406
  40.1 13.7 %collective-permute-start.2 = (bf16[1024,256]{1,0:T(8,128)(2,1)S(1)}, bf16[1024,256]{1,0:T(8,128)(2,1)S(1)}, u32[]{:S(2)}, u32[]{:S(2)}) collective-permute-start(bf16[1024,256]{1,0:T(8,128)(2,1)S(1)} %bitcast.16), channel_id=1, source_target_pairs={{0,3},{1,0},{2,1},{3,2},{4,7},{5,4},{6,5},{7,6},{8,11},{9,8},{10,9... | collective-permute-start | bytes 1572872 | tf_op jit(solution)/shard_map/ppermute | solution.py:416
  42.9 14.4 %collective-permute-start = (bf16[1024,256]{1,0:T(8,128)(2,1)S(1)}, bf16[1024,256]{1,0:T(8,128)(2,1)S(1)}, u32[]{:S(2)}, u32[]{:S(2)}) collective-permute-start(bf16[1024,256]{1,0:T(8,128)(2,1)S(1)} %bitcast.17), channel_id=1, source_target_pairs={{0,1},{1,2},{2,3},{3,0},{4,5},{5,6},{6,7},{7,4},{8,9},{9,10},{10,1... | collective-permute-start | bytes 1572872 | tf_op jit(solution)/shard_map/ppermute | solution.py:416
  53.7 11.1 %copy-start.3 = (bf16[1024,256]{1,0:T(8,128)(2,1)}, bf16[1024,256]{1,0:T(8,128)(2,1)S(1)}, u32[]{:S(2)}) copy-start(bf16[1024,256]{1,0:T(8,128)(2,1)S(1)} %collective-permute-done.2.refs_4_) | copy-start | bytes 1572868
  53.7 8.7 %collective-permute-start.3 = (bf16[512,256]{1,0:T(8,128)(2,1)S(1)}, bf16[512,256]{1,0:T(8,128)(2,1)S(1)}, u32[]{:S(2)}, u32[]{:S(2)}) collective-permute-start(bf16[512,256]{1,0:T(8,128)(2,1)S(1)} %slice.17), channel_id=1, source_target_pairs={{0,3},{1,0},{2,1},{3,2},{4,7},{5,4},{6,5},{7,6},{8,11},{9,8},{10,9... | collective-permute-start | bytes 786440 | tf_op jit(solution)/shard_map/ppermute | solution.py:416
  57.2 7.5 %copy-start.4 = (bf16[1024,256]{1,0:T(8,128)(2,1)}, bf16[1024,256]{1,0:T(8,128)(2,1)S(1)}, u32[]{:S(2)}) copy-start(bf16[1024,256]{1,0:T(8,128)(2,1)S(1)} %collective-permute-done.refs_1_) | copy-start | bytes 1572868
  57.3 7.5 %collective-permute-start.1 = (bf16[512,256]{1,0:T(8,128)(2,1)S(1)}, bf16[512,256]{1,0:T(8,128)(2,1)S(1)}, u32[]{:S(2)}, u32[]{:S(2)}) collective-permute-start(bf16[512,256]{1,0:T(8,128)(2,1)S(1)} %slice.16), channel_id=1, source_target_pairs={{0,1},{1,2},{2,3},{3,0},{4,5},{5,6},{6,7},{7,4},{8,9},{9,10},{10,1... | collective-permute-start | bytes 786440 | tf_op jit(solution)/shard_map/ppermute | solution.py:416
  57.8 29.5 %copy-start = (bf16[64,16,256]{2,1,0:T(8,128)(2,1)}, bf16[64,16,256]{2,1,0:T(8,128)(2,1)S(1)}, u32[]{:S(2)}) copy-start(bf16[64,16,256]{2,1,0:T(8,128)(2,1)S(1)} %all-to-all-done.1) | copy-start | bytes 1572868
  57.8 15.0 %collective-permute-start.12 = (bf16[1024,256]{1,0:T(8,128)(2,1)S(1)}, bf16[1024,256]{1,0:T(8,128)(2,1)S(1)}, u32[]{:S(2)}, u32[]{:S(2)}) collective-permute-start(bf16[1024,256]{1,0:T(8,128)(2,1)S(1)} %bitcast.9), channel_id=1, source_target_pairs={{0,3},{1,0},{2,1},{3,2},{4,7},{5,4},{6,5},{7,6},{8,11},{9,8},{10,9... | collective-permute-start | bytes 1572872 | tf_op jit(solution)/shard_map/ppermute | solution.py:416
  60.5 15.9 %collective-permute-start.10 = (bf16[1024,256]{1,0:T(8,128)(2,1)S(1)}, bf16[1024,256]{1,0:T(8,128)(2,1)S(1)}, u32[]{:S(2)}, u32[]{:S(2)}) collective-permute-start(bf16[1024,256]{1,0:T(8,128)(2,1)S(1)} %bitcast.10), channel_id=1, source_target_pairs={{0,1},{1,2},{2,3},{3,0},{4,5},{5,6},{6,7},{7,4},{8,9},{9,10},{10,1... | collective-permute-start | bytes 1572872 | tf_op jit(solution)/shard_map/ppermute | solution.py:416
  62.4 6.3 %copy-start.7 = (bf16[512,256]{1,0:T(8,128)(2,1)}, bf16[512,256]{1,0:T(8,128)(2,1)S(1)}, u32[]{:S(2)}) copy-start(bf16[512,256]{1,0:T(8,128)(2,1)S(1)} %collective-permute-done.3.refs_3_) | copy-start | bytes 786436
  64.8 4.0 %copy-start.8 = (bf16[512,256]{1,0:T(8,128)(2,1)}, bf16[512,256]{1,0:T(8,128)(2,1)S(1)}, u32[]{:S(2)}) copy-start(bf16[512,256]{1,0:T(8,128)(2,1)S(1)} %collective-permute-done.1.refs_2_) | copy-start | bytes 786436
  68.8 1.0 copy-start.16
  69.8 8.6 %collective-permute-start.5 = (bf16[512,256]{1,0:T(8,128)(2,1)S(1)}, bf16[512,256]{1,0:T(8,128)(2,1)S(1)}, u32[]{:S(2)}, u32[]{:S(2)}) collective-permute-start(bf16[512,256]{1,0:T(8,128)(2,1)S(1)} %get-tuple-element.53), channel_id=1, source_target_pairs={{0,3},{1,0},{2,1},{3,2},{4,7},{5,4},{6,5},{7,6},{8,11},{9,8},{10,9... | collective-permute-start | bytes 786440 | tf_op jit(solution)/shard_map/ppermute | solution.py:416
  70.2 11.7 %collective-permute-start.8 = (bf16[512,256]{1,0:T(8,128)(2,1)S(1)}, bf16[512,256]{1,0:T(8,128)(2,1)S(1)}, u32[]{:S(2)}, u32[]{:S(2)}) collective-permute-start(bf16[512,256]{1,0:T(8,128)(2,1)S(1)} %get-tuple-element.57), channel_id=1, source_target_pairs={{0,1},{1,2},{2,3},{3,0},{4,5},{5,6},{6,7},{7,4},{8,9},{9,10},{10,1... | collective-permute-start | bytes 786440 | tf_op jit(solution)/shard_map/ppermute | solution.py:416
  72.8 18.1 %copy-start.5 = (bf16[1024,256]{1,0:T(8,128)(2,1)}, bf16[1024,256]{1,0:T(8,128)(2,1)S(1)}, u32[]{:S(2)}) copy-start(bf16[1024,256]{1,0:T(8,128)(2,1)S(1)} %collective-permute-done.12.refs_4_.refs_9_) | copy-start | bytes 1572868
  72.8 11.2 %collective-permute-start.13 = (bf16[512,256]{1,0:T(8,128)(2,1)S(1)}, bf16[512,256]{1,0:T(8,128)(2,1)S(1)}, u32[]{:S(2)}, u32[]{:S(2)}) collective-permute-start(bf16[512,256]{1,0:T(8,128)(2,1)S(1)} %slice.19), channel_id=1, source_target_pairs={{0,3},{1,0},{2,1},{3,2},{4,7},{5,4},{6,5},{7,6},{8,11},{9,8},{10,9... | collective-permute-start | bytes 786440 | tf_op jit(solution)/shard_map/ppermute | solution.py:416
  76.5 14.5 %copy-start.6 = (bf16[1024,256]{1,0:T(8,128)(2,1)}, bf16[1024,256]{1,0:T(8,128)(2,1)S(1)}, u32[]{:S(2)}) copy-start(bf16[1024,256]{1,0:T(8,128)(2,1)S(1)} %collective-permute-done.10.refs_1_.refs_6_) | copy-start | bytes 1572868
  76.5 10.8 %collective-permute-start.11 = (bf16[512,256]{1,0:T(8,128)(2,1)S(1)}, bf16[512,256]{1,0:T(8,128)(2,1)S(1)}, u32[]{:S(2)}, u32[]{:S(2)}) collective-permute-start(bf16[512,256]{1,0:T(8,128)(2,1)S(1)} %slice.18), channel_id=1, source_target_pairs={{0,1},{1,2},{2,3},{3,0},{4,5},{5,6},{6,7},{7,4},{8,9},{9,10},{10,1... | collective-permute-start | bytes 786440 | tf_op jit(solution)/shard_map/ppermute | solution.py:416
  76.6 16.3 %collective-permute-start.4 = (bf16[512,256]{1,0:T(8,128)(2,1)S(1)}, bf16[512,256]{1,0:T(8,128)(2,1)S(1)}, u32[]{:S(2)}, u32[]{:S(2)}) collective-permute-start(bf16[512,256]{1,0:T(8,128)(2,1)S(1)} %get-tuple-element.51), channel_id=1, source_target_pairs={{0,1},{1,2},{2,3},{3,0},{4,5},{5,6},{6,7},{7,4},{8,9},{9,10},{10,1... | collective-permute-start | bytes 786440 | tf_op jit(solution)/shard_map/ppermute | solution.py:416
  78.4 14.5 %collective-permute-start.7 = (bf16[512,256]{1,0:T(8,128)(2,1)S(1)}, bf16[512,256]{1,0:T(8,128)(2,1)S(1)}, u32[]{:S(2)}, u32[]{:S(2)}) collective-permute-start(bf16[512,256]{1,0:T(8,128)(2,1)S(1)} %get-tuple-element.55), channel_id=1, source_target_pairs={{0,3},{1,0},{2,1},{3,2},{4,7},{5,4},{6,5},{7,6},{8,11},{9,8},{10,9... | collective-permute-start | bytes 786440 | tf_op jit(solution)/shard_map/ppermute | solution.py:416
  81.9 13.4 %collective-permute-start.6 = (bf16[512,256]{1,0:T(8,128)(2,1)S(1)}, bf16[512,256]{1,0:T(8,128)(2,1)S(1)}, u32[]{:S(2)}, u32[]{:S(2)}) collective-permute-start(bf16[512,256]{1,0:T(8,128)(2,1)S(1)} %add_convert_fusion.3), channel_id=1, source_target_pairs={{0,3},{1,0},{2,1},{3,2},{4,7},{5,4},{6,5},{7,6},{8,11},{9,8},{10,9... | collective-permute-start | bytes 786440 | tf_op jit(solution)/shard_map/ppermute | solution.py:416
  84.0 6.9 %copy-start.9 = (bf16[512,256]{1,0:T(8,128)(2,1)}, bf16[512,256]{1,0:T(8,128)(2,1)S(1)}, u32[]{:S(2)}) copy-start(bf16[512,256]{1,0:T(8,128)(2,1)S(1)} %collective-permute-done.13.refs_3_.refs_8_) | copy-start | bytes 786436
  84.0 14.5 %collective-permute-start.9 = (bf16[512,256]{1,0:T(8,128)(2,1)S(1)}, bf16[512,256]{1,0:T(8,128)(2,1)S(1)}, u32[]{:S(2)}, u32[]{:S(2)}) collective-permute-start(bf16[512,256]{1,0:T(8,128)(2,1)S(1)} %add_convert_fusion.2), channel_id=1, source_target_pairs={{0,1},{1,2},{2,3},{3,0},{4,5},{5,6},{6,7},{7,4},{8,9},{9,10},{10,1... | collective-permute-start | bytes 786440 | tf_op jit(solution)/shard_map/ppermute | solution.py:416
  87.2 3.7 %copy-start.10 = (bf16[512,256]{1,0:T(8,128)(2,1)}, bf16[512,256]{1,0:T(8,128)(2,1)S(1)}, u32[]{:S(2)}) copy-start(bf16[512,256]{1,0:T(8,128)(2,1)S(1)} %collective-permute-done.11.refs_2_.refs_7_) | copy-start | bytes 786436
  90.9 1.0 copy-start.15
  91.9 7.6 %copy-start.11 = (bf16[512,256]{1,0:T(8,128)(2,1)}, bf16[512,256]{1,0:T(8,128)(2,1)S(1)}, u32[]{:S(2)}) copy-start(bf16[512,256]{1,0:T(8,128)(2,1)S(1)} %get-tuple-element.69) | copy-start | bytes 786436
  91.9 7.6 %copy-start.12 = (bf16[512,256]{1,0:T(8,128)(2,1)}, bf16[512,256]{1,0:T(8,128)(2,1)S(1)}, u32[]{:S(2)}) copy-start(bf16[512,256]{1,0:T(8,128)(2,1)S(1)} %get-tuple-element.65) | copy-start | bytes 786436
  91.9 7.6 %copy-start.14 = (bf16[1024,512]{1,0:T(8,128)(2,1)}, bf16[1024,512]{1,0:T(8,128)(2,1)S(1)}, u32[]{:S(2)}) copy-start(bf16[1024,512]{1,0:T(8,128)(2,1)S(1)} %get-tuple-element.74.refs_11_) | copy-start | bytes 3145732
  99.6 34.4 %all-to-all-start.2 = ((bf16[64,16,256]{2,1,0:T(8,128)(2,1)}), bf16[64,16,256]{2,1,0:T(8,128)(2,1)S(1)}, u32[]{:S(2)}, u32[]{:S(2)}) async-start(bf16[64,16,256]{2,1,0:T(8,128)(2,1)} %bitcast.5), calls=%async_computation.2 | async-start | bytes 1048576 | tf_op jit(solution)/shard_map/all_to_all | solution.py:406
  112.1 7.7 %collective-permute-start.15 = (bf16[512,256]{1,0:T(8,128)(2,1)}, bf16[512,256]{1,0:T(8,128)(2,1)S(1)}, u32[]{:S(2)}, u32[]{:S(2)}) collective-permute-start(bf16[512,256]{1,0:T(8,128)(2,1)} %copy-done.12), channel_id=1, source_target_pairs={{0,3},{1,0},{2,1},{3,2},{4,7},{5,4},{6,5},{7,6},{8,11},{9,8},{10,9... | collective-permute-start | bytes 786440 | tf_op jit(solution)/shard_map/ppermute | solution.py:416
  112.2 9.1 %collective-permute-start.18 = (bf16[512,256]{1,0:T(8,128)(2,1)}, bf16[512,256]{1,0:T(8,128)(2,1)S(1)}, u32[]{:S(2)}, u32[]{:S(2)}) collective-permute-start(bf16[512,256]{1,0:T(8,128)(2,1)} %copy-done.11), channel_id=1, source_target_pairs={{0,1},{1,2},{2,3},{3,0},{4,5},{5,6},{6,7},{7,4},{8,9},{9,10},{10,1... | collective-permute-start | bytes 786440 | tf_op jit(solution)/shard_map/ppermute | solution.py:416
  113.7 13.0 %collective-permute-start.14 = (bf16[512,256]{1,0:T(8,128)(2,1)S(1)}, bf16[512,256]{1,0:T(8,128)(2,1)S(1)}, u32[]{:S(2)}, u32[]{:S(2)}) collective-permute-start(bf16[512,256]{1,0:T(8,128)(2,1)S(1)} %get-tuple-element.63), channel_id=1, source_target_pairs={{0,1},{1,2},{2,3},{3,0},{4,5},{5,6},{6,7},{7,4},{8,9},{9,10},{10,1... | collective-permute-start | bytes 786440 | tf_op jit(solution)/shard_map/ppermute | solution.py:416
  113.7 13.0 %collective-permute-start.17 = (bf16[512,256]{1,0:T(8,128)(2,1)S(1)}, bf16[512,256]{1,0:T(8,128)(2,1)S(1)}, u32[]{:S(2)}, u32[]{:S(2)}) collective-permute-start(bf16[512,256]{1,0:T(8,128)(2,1)S(1)} %get-tuple-element.67), channel_id=1, source_target_pairs={{0,3},{1,0},{2,1},{3,2},{4,7},{5,4},{6,5},{7,6},{8,11},{9,8},{10,9... | collective-permute-start | bytes 786440 | tf_op jit(solution)/shard_map/ppermute | solution.py:416
  119.8 25.5 %copy-start.2 = (f32[256,8]{1,0:T(8,128)S(1)}, f32[256,8]{1,0:T(8,128)}, u32[]{:S(2)}) copy-start(f32[256,8]{1,0:T(8,128)} %get-tuple-element.44.info) | copy-start | bytes 24580
  119.9 11.2 %collective-permute-start.16 = (bf16[512,256]{1,0:T(8,128)(2,1)S(1)}, bf16[512,256]{1,0:T(8,128)(2,1)S(1)}, u32[]{:S(2)}, u32[]{:S(2)}) collective-permute-start(bf16[512,256]{1,0:T(8,128)(2,1)S(1)} %add_convert_fusion.1), channel_id=1, source_target_pairs={{0,3},{1,0},{2,1},{3,2},{4,7},{5,4},{6,5},{7,6},{8,11},{9,8},{10,9... | collective-permute-start | bytes 786440 | tf_op jit(solution)/shard_map/ppermute | solution.py:416
  121.4 10.9 %collective-permute-start.19 = (bf16[512,256]{1,0:T(8,128)(2,1)S(1)}, bf16[512,256]{1,0:T(8,128)(2,1)S(1)}, u32[]{:S(2)}, u32[]{:S(2)}) collective-permute-start(bf16[512,256]{1,0:T(8,128)(2,1)S(1)} %add_convert_fusion), channel_id=1, source_target_pairs={{0,1},{1,2},{2,3},{3,0},{4,5},{5,6},{6,7},{7,4},{8,9},{9,10},{10,1... | collective-permute-start | bytes 786440 | tf_op jit(solution)/shard_map/ppermute | solution.py:416
  133.4 0.6 copy-start.13
  134.0 29.1 %all-to-all-start.3 = ((bf16[64,16,256]{2,1,0:T(8,128)(2,1)}), bf16[64,16,256]{2,1,0:T(8,128)(2,1)S(1)}, u32[]{:S(2)}, u32[]{:S(2)}) async-start(bf16[64,16,256]{2,1,0:T(8,128)(2,1)} %bitcast.7), calls=%async_computation.3 | async-start | bytes 1048576 | tf_op jit(solution)/shard_map/all_to_all | solution.py:406
  146.5 11.6 %collective-permute-start.22 = (bf16[256,256]{1,0:T(8,128)(2,1)S(1)}, bf16[256,256]{1,0:T(8,128)(2,1)S(1)}, u32[]{:S(2)}, u32[]{:S(2)}) collective-permute-start(bf16[256,256]{1,0:T(8,128)(2,1)S(1)} %combine.2.refs_0_), channel_id=1, source_target_pairs={{0,3},{1,0},{2,1},{3,2},{4,7},{5,4},{6,5},{7,6},{8,11},{9,8},{10,9... | collective-permute-start | bytes 393224 | tf_op jit(solution)/shard_map/ppermute | solution.py:416
  146.6 11.5 %collective-permute-start.21 = (bf16[256,256]{1,0:T(8,128)(2,1)S(1)}, bf16[256,256]{1,0:T(8,128)(2,1)S(1)}, u32[]{:S(2)}, u32[]{:S(2)}) collective-permute-start(bf16[256,256]{1,0:T(8,128)(2,1)S(1)} %combine.2.refs_0_), channel_id=1, source_target_pairs={{0,2},{1,3},{2,0},{3,1},{4,6},{5,7},{6,4},{7,5},{8,10},{9,11},{10,... | collective-permute-start | bytes 393224 | tf_op jit(solution)/shard_map/ppermute | solution.py:416
  148.5 9.6 %collective-permute-start.20 = (bf16[256,256]{1,0:T(8,128)(2,1)S(1)}, bf16[256,256]{1,0:T(8,128)(2,1)S(1)}, u32[]{:S(2)}, u32[]{:S(2)}) collective-permute-start(bf16[256,256]{1,0:T(8,128)(2,1)S(1)} %combine.2.refs_0_), channel_id=1, source_target_pairs={{0,1},{1,2},{2,3},{3,0},{4,5},{5,6},{6,7},{7,4},{8,9},{9,10},{10,1... | collective-permute-start | bytes 393224 | tf_op jit(solution)/shard_map/ppermute | solution.py:416
  164.7 4.8 %collective-permute-start.25 = (bf16[256,256]{1,0:T(8,128)(2,1)S(1)}, bf16[256,256]{1,0:T(8,128)(2,1)S(1)}, u32[]{:S(2)}, u32[]{:S(2)}) collective-permute-start(bf16[256,256]{1,0:T(8,128)(2,1)S(1)} %combine.3.refs_0_), channel_id=1, source_target_pairs={{0,3},{1,0},{2,1},{3,2},{4,7},{5,4},{6,5},{7,6},{8,11},{9,8},{10,9... | collective-permute-start | bytes 393224 | tf_op jit(solution)/shard_map/ppermute | solution.py:416
  164.8 6.0 %collective-permute-start.24 = (bf16[256,256]{1,0:T(8,128)(2,1)S(1)}, bf16[256,256]{1,0:T(8,128)(2,1)S(1)}, u32[]{:S(2)}, u32[]{:S(2)}) collective-permute-start(bf16[256,256]{1,0:T(8,128)(2,1)S(1)} %combine.3.refs_0_), channel_id=1, source_target_pairs={{0,2},{1,3},{2,0},{3,1},{4,6},{5,7},{6,4},{7,5},{8,10},{9,11},{10,... | collective-permute-start | bytes 393224 | tf_op jit(solution)/shard_map/ppermute | solution.py:416
  166.8 7.4 %collective-permute-start.23 = (bf16[256,256]{1,0:T(8,128)(2,1)S(1)}, bf16[256,256]{1,0:T(8,128)(2,1)S(1)}, u32[]{:S(2)}, u32[]{:S(2)}) collective-permute-start(bf16[256,256]{1,0:T(8,128)(2,1)S(1)} %combine.3.refs_0_), channel_id=1, source_target_pairs={{0,1},{1,2},{2,3},{3,0},{4,5},{5,6},{6,7},{7,4},{8,9},{9,10},{10,1... | collective-permute-start | bytes 393224 | tf_op jit(solution)/shard_map/ppermute | solution.py:416
